TPU v7x, 32 devices: a whole 2x2x4 slice. The times are simulated.
32 devices in a mesh: slab: 4 (over x, core), rot: 8 (over z, y).
Axes of the slice: x: 2, y: 2, z: 4, core: 2. Of those that a mesh axis runs over, the one named last changes fastest.
Arguments:
- tomogram: bfloat16 [96, 128, 128], P('slab'), may hold values from -50 to 50
- templates: bfloat16 [16, 48, 2304], P('rot'), may hold values from -0.01953125 to 0.01953125
- rotation_ids: int32 [16], P('rot'), may hold values from 0 to 15, each once
Outputs:
- best_score: float32 [96, 128, 128], P('slab', 'rot')
- orientation: float32 [96, 128, 128], P('slab', 'rot')
Inputs may be any that keep to these rules, and one draw needn't show every extreme that they name: `rotation_ids`: each rotation index 0 .. 15 appears once.
All inputs are finite; a program needn't handle non-finite values.
Results may differ from a plain program's by a relative error of at most 0.025.
Values may be sent and summed in bfloat16 or wider, within the bound.
A program may use at most 128 MiB of HBM per device.

v0:
```python
import math

import jax
import jax.numpy as jnp
from jax import lax
from jax.sharding import PartitionSpec as P

TMPL = 48


def extended(array, sides, width):
    for axis, dim in sides:
        size, length = (lax.axis_size(axis), array.shape[dim])
        up = [(i, (i + 1) % size) for i in range(size - 1)]
        down = [(j, i) for i, j in up]
        last = lax.slice_in_dim(array, length - width, length, axis=dim)
        leading = lax.slice_in_dim(array, 0, width, axis=dim)
        before = lax.ppermute(last, axis, up)
        after = lax.ppermute(leading, axis, down)
        array = jnp.concatenate([before, array, after], axis=dim)
    return array


def angle_table(length, count, shift):
    frequency = jnp.arange(length, dtype=jnp.int32)[:, None]
    position = jnp.arange(count, dtype=jnp.int32)[None, :] - shift
    phase = jnp.mod(frequency * position, length).astype(jnp.float32) * (2.0 * math.pi / length)
    return (jnp.cos(phase).astype(jnp.bfloat16), jnp.sin(phase).astype(jnp.bfloat16))


def forward_pair(cosine, sine):
    return jnp.stack([jnp.stack([cosine, sine]), jnp.stack([-sine, cosine])])


def backward_pair(cosine, sine):
    return jnp.stack([jnp.stack([cosine, -sine]), jnp.stack([sine, cosine])])


def product_of(form, left, right):
    return jnp.einsum(form, left, right, preferred_element_type=jnp.float32)


def exact_product(form, left, right):
    return jnp.einsum(
        form, left, right, precision=lax.Precision.HIGHEST, preferred_element_type=jnp.float32
    )


def on_device(tomogram, templates, rotation_ids):
    slab_depth = tomogram.shape[0]
    window = tomogram.shape[1]
    half_width = TMPL // 2
    padded_depth = slab_depth + TMPL
    padded = extended(tomogram, (("slab", 0),), half_width)
    cos_window, sin_window = angle_table(window, window, 0)
    real_pair = jnp.stack([cos_window, -sin_window])
    forward_rows = forward_pair(cos_window, sin_window)
    cos_depth, sin_depth = angle_table(padded_depth, padded_depth, 0)
    plane_size = 8
    plane_groups = padded_depth // plane_size
    row_size = 32
    row_groups = window // row_size
    forward_split = forward_pair(cos_depth, sin_depth).reshape(
        2, 2, padded_depth, plane_groups, plane_size
    )
    inverse_depth = backward_pair(
        cos_depth[half_width : half_width + slab_depth],
        sin_depth[half_width : half_width + slab_depth],
    )
    inverse_split = backward_pair(cos_window, sin_window).reshape(
        2, 2, window, row_groups, row_size
    )
    cos_shift, sin_shift = angle_table(padded_depth, TMPL, half_width)
    template_depth = jnp.stack([cos_shift, sin_shift])
    cos_cube, sin_cube = angle_table(window, TMPL, half_width)
    template_plane = backward_pair(cos_cube, sin_cube)
    plane_rows = template_plane.reshape(2, 2, row_groups, row_size, TMPL)

    def plane_step(plane_block):
        after_columns = product_of("pyx,okx->opyk", plane_block, real_pair).astype(jnp.bfloat16)
        return product_of("ipyx,oiky->opkx", after_columns, forward_rows).astype(jnp.bfloat16)

    planar = lax.map(plane_step, padded.reshape(plane_groups, plane_size, window, window))

    def column_step(group_number):
        rows_part = lax.dynamic_slice_in_dim(planar, group_number * row_size, row_size, 3)
        return product_of("nipyx,oiknp->okyx", rows_part, forward_split).astype(jnp.bfloat16)

    spectrum = lax.map(column_step, jnp.arange(row_groups, dtype=jnp.int32))
    slice_out = jnp.arange(slab_depth, dtype=jnp.int32)[:, None]
    slice_in = jnp.arange(padded_depth, dtype=jnp.int32)[None, :]
    box_depth = ((slice_in - slice_out >= 0) & (slice_in - slice_out < TMPL)).astype(jnp.float32)
    cell_out = jnp.arange(window, dtype=jnp.int32)[:, None]
    cell_in = jnp.arange(window, dtype=jnp.int32)[None, :]
    box_window = (jnp.mod(cell_in - cell_out + half_width, window) < TMPL).astype(jnp.float32)
    squares = jnp.square(padded.astype(jnp.float32))
    energy = exact_product("qp,pyx->qyx", box_depth, squares)
    energy = exact_product("yn,qnx->qyx", box_window, energy)
    energy = exact_product("xn,qyn->qyx", box_window, energy)
    divisor = padded_depth * window * window * jnp.sqrt(energy / TMPL**3 + 1e-05)

    def one_rotation(template):
        template_cube = template.reshape(TMPL, TMPL, TMPL)
        template_z = product_of("abc,oka->okbc", template_cube, template_depth).astype(jnp.bfloat16)
        template_zx = product_of("ipbc,oikc->opbk", template_z, template_plane).astype(jnp.bfloat16)

        def row_step(group_number):
            spectrum_rows = lax.dynamic_index_in_dim(spectrum, group_number, 0, keepdims=False)
            table_rows = lax.dynamic_index_in_dim(plane_rows, group_number, 2, keepdims=False)
            template_rows = product_of("ipbk,oijb->opjk", template_zx, table_rows).astype(
                jnp.bfloat16
            )
            spectrum_real = spectrum_rows[0].astype(jnp.float32)
            spectrum_imag = spectrum_rows[1].astype(jnp.float32)
            template_real = template_rows[0].astype(jnp.float32)
            template_imag = template_rows[1].astype(jnp.float32)
            product = jnp.stack(
                [
                    spectrum_real * template_real - spectrum_imag * template_imag,
                    spectrum_real * template_imag + spectrum_imag * template_real,
                ]
            ).astype(jnp.bfloat16)
            return product_of("ikyx,oiqk->oqyx", product, inverse_depth).astype(jnp.bfloat16)

        inverse_parts = lax.map(row_step, jnp.arange(row_groups, dtype=jnp.int32))
        inverse_zy = product_of("niqbx,oiynb->oqyx", inverse_parts, inverse_split).astype(
            jnp.bfloat16
        )
        correlation = product_of("iqyk,ixk->qyx", inverse_zy, real_pair)
        return correlation / divisor

    scores = lax.map(one_rotation, templates)
    rotation_total = templates.shape[0] * lax.axis_size("rot")
    band_rows = window // lax.axis_size("rot")
    factors = 1.0 - (2.0 * rotation_ids.astype(jnp.float32) + 1.0) / rotation_total
    local_best = jnp.max(scores, axis=0)
    best_score = lax.pmax(local_best.astype(jnp.bfloat16), "rot").astype(local_best.dtype)
    weight = jnp.square(jnp.maximum(scores - best_score + 1.0, 0.0))
    weight_total = jnp.sum(weight, axis=0)
    moment = jnp.sum(weight * factors[:, None, None, None], axis=0)
    total_band, moment_band = (
        lax.psum_scatter(
            weight_total.astype(jnp.bfloat16), "rot", scatter_dimension=1, tiled=True
        ).astype(jnp.float32),
        lax.psum_scatter(
            moment.astype(jnp.bfloat16), "rot", scatter_dimension=1, tiled=True
        ).astype(jnp.float32),
    )
    band_start = lax.axis_index("rot") * band_rows
    best_band = lax.dynamic_slice_in_dim(best_score, band_start, band_rows, 1)
    orientation = moment_band / total_band
    return (best_band, orientation)


def solution(mesh):
    return jax.shard_map(
        on_device,
        mesh=mesh,
        in_specs=(P("slab", None, None), P("rot", None, None), P("rot")),
        out_specs=(P("slab", "rot", None), P("slab", "rot", None)),
        check_vma=False,
    )
```

profile of v0, /device:TPU:13, one launch (start us, length us, event | category | flops | bytes accessed | tf_op | source)
XLA Modules:
  0.0 385.6 jit_solution(12617786192422805329)
XLA Ops:
  7.2 3.7 collective-permute-start
  21.5 3.0 collective-permute-done.1
  25.8 2.8 convert_multiply_fusion.4
  28.6 19.5 %while.45 = (s32[]{:T(128)}, bf16[9,2,8,128,128]{3,4,1,2,0:T(8,128)(2,1)}, bf16[9,8,128,128]{3,2,1,0:T(8,128)(2,1)S(1)}, bf16[2,128,128]{2,1,0:T(8,128)(2,1)}, bf16[2,2,128,128]{3,2,1,0:T(8,128)(2,1)S(1)}) while((s32[]{:T(128)}, bf16[9,2,8,128,128]{3,4,1,2,0:T(8,128)(2,1)}, bf16[9,8,128,128]{3,2,1,0:T(8,128)(2,1)S(1)}, ...), condition=%wide.region_1.2_spmd.clone, body=%wide.region_0.1_spmd.sunk.clone | while | flops 201850880 | bytes 984125 | solution.py:83
  28.6 2.2 fusion.192
  30.8 2.2 fusion.192
  33.0 2.2 fusion.192
  35.2 2.2 fusion.192
  37.3 2.2 fusion.192
  39.5 2.2 fusion.192
  41.6 2.2 fusion.192
  43.8 2.2 fusion.192
  46.0 2.2 fusion.192
  48.2 12.3 %copy.9 = bf16[9,2,8,128,128]{4,0,2,1,3:T(8,128)(2,1)} copy(bf16[9,2,8,128,128]{3,4,1,2,0:T(8,128)(2,1)} %get-tuple-element.172) | data formatting | bytes 9437184 | tf_op jit(solution)/shard_map/while | solution.py:89
  60.5 18.2 %while.46 = (s32[]{:T(128)}, bf16[4,2,72,32,128]{4,3,2,1,0:T(8,128)(2,1)}, s32[4]{0:T(128)S(1)}, bf16[9,2,8,128,128]{4,0,2,1,3:T(8,128)(2,1)}, bf16[2,2,72,9,8]{2,3,4,1,0:T(8,128)(2,1)S(1)}, /*index=5*/s32[1]{0:T(128)}) while((s32[]{:T(128)}, bf16[4,2,72,32,128]{4,3,2,1,0:T(8,128)(2,1)}, s32[4]{0:T(128)S(1)}, ...), condition=%wide.region_3.4_spmd.clone, body=%wide.region_2.3_spmd.sunk.clone | while | flops 170459136 | bytes 5678211 | solution.py:89
  61.6 2.1 fusion.195
  66.2 2.1 fusion.195
  70.7 2.1 fusion.195
  75.2 2.1 fusion.195
  78.7 6.4 %fusion.57 = f32[24,128,128]{2,0,1:T(8,128)S(1)} fusion(f32[72,128,128]{2,1,0:T(8,128)} %convert_multiply_fusion.4), kind=kOutput, calls=%fused_computation.58 | convolution fusion | flops 339745536 | bytes 6291456 | tf_op jit(solution)/shard_map/qp,pyx->qyx/dot_general | solution.py:44
  86.2 2.4 sqrt_multiply_fusion
  88.6 81.4 %while.48 = (s32[]{:T(128)}, f32[2,24,128,128]{3,2,1,0:T(8,128)}, bf16[2,48,2304]{2,1,0:T(8,128)(2,1)}, bf16[2,72,48]{2,1,0:T(8,128)(2,1)S(1)}, bf16[2,2,128,48]...) while((s32[]{:T(128)}, f32[2,24,128,128]{3,2,1,0:T(8,128)}, ...), condition=%wide.region_7.8_spmd.clone, body=%wide.region_4.7_spmd.sunk.clone | while | flops 982880256 | bytes 22993444 | solution.py:132
  91.3 2.1 copy.75
  95.0 30.1 %while.47 = (s32[]{:T(128)}, bf16[4,2,24,32,128]{4,2,1,3,0:T(8,128)(2,1)}, s32[4]{0:T(128)S(1)}, bf16[4,2,72,32,128]{4,3,2,1,0:T(8,128)(2,1)}, bf16[2,2,4,32,48]...) while((s32[]{:T(128)}, ...), condition=%wide.region_6.6_spmd, body=%wide.region_5.5_spmd.sunk | while | flops 174784512 | bytes 10522831 | solution.py:125
  125.1 4.2 %bitcast_dynamic-update-slice_fusion.3 = f32[2,24,128,128]{3,2,1,0:T(8,128)} fusion(f32[2,24,128,128]{3,2,1,0:T(8,128)} %get-tuple-element.608, s32[]{:T(128)} %get-tuple-element.607, f32[24,128,128]{2,1,0:T(8,128)} %get-tuple-element.632, bf16[4,2,24,32,128,1]{4,2,1,3,0,5:T(8,128)(2,1)} %bitcast.290, ...), kind=kOutput, calls=%fused_computation.45.clone.1.clone | convolution fusion | flops 605159424 | bytes 4915712 | tf_op jit(solution)/shard_map/while/body/eval_jaxpr/iqyk,ixk->qyx/dot_general | solution.py:40
  132.0 2.1 copy.75
  135.7 30.0 %while.47 = (s32[]{:T(128)}, bf16[4,2,24,32,128]{4,2,1,3,0:T(8,128)(2,1)}, s32[4]{0:T(128)S(1)}, bf16[4,2,72,32,128]{4,3,2,1,0:T(8,128)(2,1)}, bf16[2,2,4,32,48]...) while((s32[]{:T(128)}, ...), condition=%wide.region_6.6_spmd, body=%wide.region_5.5_spmd.sunk | while | flops 174784512 | bytes 10522831 | solution.py:125
  165.7 4.2 %bitcast_dynamic-update-slice_fusion.3 = f32[2,24,128,128]{3,2,1,0:T(8,128)} fusion(f32[2,24,128,128]{3,2,1,0:T(8,128)} %get-tuple-element.608, s32[]{:T(128)} %get-tuple-element.607, f32[24,128,128]{2,1,0:T(8,128)} %get-tuple-element.632, bf16[4,2,24,32,128,1]{4,2,1,3,0,5:T(8,128)(2,1)} %bitcast.290, ...), kind=kOutput, calls=%fused_computation.45.clone.1.clone | convolution fusion | flops 605159424 | bytes 4915712 | tf_op jit(solution)/shard_map/while/body/eval_jaxpr/iqyk,ixk->qyx/dot_general | solution.py:40
  170.0 3.3 reduce_max.9
  173.4 72.5 %all-reduce.2.cloned.1.call-done = bf16[24,128,128]{2,1,0:T(8,128)(2,1)} async-done(((bf16[24,128,128]{2,1,0:T(8,128)(2,1)}), bf16[24,128,128]{2,1,0:T(8,128)(2,1)}) %all-reduce.2.cloned.1.call-update) | async-done | bytes 786448 | tf_op jit(solution)/shard_map/pmax | solution.py:137
  251.7 60.3 %reduce-scatter.3.cloned.1.call-done = bf16[24,16,128]{2,1,0:T(8,128)(2,1)} async-done(((bf16[24,128,128]{2,1,0:T(8,128)(2,1)}), bf16[24,16,128]{2,1,0:T(8,128)(2,1)}) %reduce-scatter.3.cloned.1.call-update) | async-done | bytes 98320 | tf_op jit(solution)/shard_map/reduce_scatter | solution.py:145
  312.0 65.4 %reduce-scatter.5.cloned.1.call-done = bf16[24,16,128]{2,1,0:T(8,128)(2,1)} async-done(((bf16[24,128,128]{2,1,0:T(8,128)(2,1)}), bf16[24,16,128]{2,1,0:T(8,128)(2,1)}) %reduce-scatter.5.cloned.1.call-update) | async-done | bytes 98320 | tf_op jit(solution)/shard_map/reduce_scatter | solution.py:142
  (148 shorter events, 80.9 us)
Async XLA Ops:
  7.2 238.7 %all-reduce.2.cloned.1.call-start = ((), (), s32[]{:S(2)}) async-start(), calls=%async_computation.2 | async-start | bytes 1572864 | tf_op jit(solution)/shard_map/pmax | solution.py:137
  7.2 13.0 %collective-permute-start = (bf16[24,128,128]{2,1,0:T(8,128)(2,1)}, bf16[24,128,128]{2,1,0:T(8,128)(2,1)}, u32[]{:S(2)}, u32[]{:S(2)}) collective-permute-start(bf16[24,128,128]{2,1,0:T(8,128)(2,1)} %param.11), channel_id=1, source_target_pairs={{0,8},{8,16},{16,24},{1,9},{9,17},{17,25},{2,10},{10,18},{18,26},{... | collective-permute-start | bytes 2359304 | tf_op jit(solution)/shard_map/ppermute | solution.py:18
  10.9 13.6 %collective-permute-start.1 = (bf16[24,128,128]{2,1,0:T(8,128)(2,1)}, bf16[24,128,128]{2,1,0:T(8,128)(2,1)}, u32[]{:S(2)}, u32[]{:S(2)}) collective-permute-start(bf16[24,128,128]{2,1,0:T(8,128)(2,1)} %param.11), channel_id=1, source_target_pairs={{8,0},{16,8},{24,16},{9,1},{17,9},{25,17},{10,2},{18,10},{26,18},{... | collective-permute-start | bytes 2359304 | tf_op jit(solution)/shard_map/ppermute | solution.py:19
  16.3 5.0 %copy-start.4 = (bf16[24,128,128]{2,1,0:T(8,128)(2,1)S(1)}, bf16[24,128,128]{2,1,0:T(8,128)(2,1)}, u32[]{:S(2)}) copy-start(bf16[24,128,128]{2,1,0:T(8,128)(2,1)} %param.11) | copy-start | bytes 2359300
  88.6 2.7 copy-start.2
  95.0 30.1 %copy-start.5 = (bf16[2,2,128,4,32]{4,3,2,1,0:T(4,128)(2,1)S(1)}, bf16[2,2,128,4,32]{4,3,2,1,0:T(4,128)(2,1)}, u32[]{:S(2)}) copy-start(bf16[2,2,128,4,32]{4,3,2,1,0:T(4,128)(2,1)} %get-tuple-element.630) | copy-start | bytes 393220 | tf_op jit(solution)/shard_map/while
  100.5 0.7 copy-start.6
  108.0 0.7 copy-start.6
  115.6 0.7 copy-start.6
  123.0 0.7 copy-start.6
  125.1 4.2 %copy-start.3 = (bf16[2,72,48]{2,1,0:T(8,128)(2,1)S(1)}, bf16[2,72,48]{2,1,0:T(8,128)(2,1)}, u32[]{:S(2)}) copy-start(bf16[2,72,48]{2,1,0:T(8,128)(2,1)} %copy-done.2) | copy-start | bytes 41476 | tf_op jit(solution)/shard_map/while
  129.3 2.7 copy-start.2
  135.6 30.1 %copy-start.5 = (bf16[2,2,128,4,32]{4,3,2,1,0:T(4,128)(2,1)S(1)}, bf16[2,2,128,4,32]{4,3,2,1,0:T(4,128)(2,1)}, u32[]{:S(2)}) copy-start(bf16[2,2,128,4,32]{4,3,2,1,0:T(4,128)(2,1)} %get-tuple-element.630) | copy-start | bytes 393220 | tf_op jit(solution)/shard_map/while
  141.2 0.7 copy-start.6
  148.7 0.7 copy-start.6
  156.2 0.7 copy-start.6
  163.7 0.7 copy-start.6
  165.7 4.3 %copy-start.3 = (bf16[2,72,48]{2,1,0:T(8,128)(2,1)S(1)}, bf16[2,72,48]{2,1,0:T(8,128)(2,1)}, u32[]{:S(2)}) copy-start(bf16[2,72,48]{2,1,0:T(8,128)(2,1)} %copy-done.2) | copy-start | bytes 41476 | tf_op jit(solution)/shard_map/while
  170.0 3.4 copy-start.7
  173.3 73.9 %copy-start = (f32[2,24,128,128]{3,2,1,0:T(8,128)S(1)}, f32[2,24,128,128]{3,2,1,0:T(8,128)}, u32[]{:S(2)}) copy-start(f32[2,24,128,128]{3,2,1,0:T(8,128)} %get-tuple-element.152) | copy-start | bytes 9437188
  173.3 138.7 %reduce-scatter.3.cloned.1.call-start = ((), (), s32[]{:S(2)}) async-start(), calls=%async_computation.3 | async-start | bytes 884736 | tf_op jit(solution)/shard_map/reduce_scatter | solution.py:145
  247.2 2.1 copy-start.1
  249.3 128.1 %reduce-scatter.5.cloned.1.call-start = ((), (), s32[]{:S(2)}) async-start(), calls=%async_computation.4 | async-start | bytes 884736 | tf_op jit(solution)/shard_map/reduce_scatter | solution.py:142
Sparse Core Ops, SparseCore 0:
  173.5 72.3 all-reduce.1
  249.6 62.3 reduce-scatter.2
  315.3 62.0 reduce-scatter.4
where the time goes:
time: 392 us; the launch traced here: 386 us
  waiting for transfers between devices  202 us (52%)
  matrix products  70.7 us (18%)
  local copies, waits for them, and re-layouts  44.2 us (11%)
  other arithmetic  31.1 us (8%)
  loops' own time  17.9 us (5%)
  between operations  14 us (4%)
  starting transfers between devices  5.73 us (1%)
    pmax x1, waiting for transfers between devices, on_device(): lax.pmax(local_best.astype(jnp.bfloat16), 'rot').astype(local_best.dtype)  72.5 us
    reduce_scatter x1, waiting for transfers between devices, on_device(): lax.psum_scatter(weight_total.astype(jnp.bfloat16), 'rot', scatter_dimens...  65.4 us
    dot_general x35, matrix products, product_of(): return jnp.einsum(form, left, right, preferred_element_type=jnp.float32)  60.8 us
    reduce_scatter x1, waiting for transfers between devices, on_device(): lax.psum_scatter(moment.astype(jnp.bfloat16), 'rot', scatter_dimension=1,...  60.3 us
    another operation x2, loops' own time, one_rotation(): inverse_parts = lax.map(row_step, jnp.arange(row_groups, dtype=jnp.int32))  15.4 us
    another operation x11, other arithmetic  13.7 us
    while x1, local copies, waits for them, and re-layouts, on_device(): spectrum = lax.map(column_step, jnp.arange(row_groups, dtype=jnp.int32))  12.3 us
    dot_general x3, matrix products, exact_product(): jnp.einsum(form, left, right, precision=lax.Precision.HIGHEST, preferred_...  9.89 us
  transfers between devices with their start and end apart: 5, of which 4 were waited for; matrix products, arithmetic and copies ran while one was open for 3% of the time, Pallas kernels for 0%

commit v1 on v0

v1 whole, which is shorter than its diff:
```python
import functools
import math

import jax
import jax.numpy as jnp
import numpy as np
from jax import lax
from jax.experimental import pallas as pl
from jax.experimental.pallas import tpu as pltpu
from jax.sharding import PartitionSpec as P

TMPL = 48
HALF = TMPL // 2
KP = 40
CUBE = 64
BF16 = jnp.bfloat16
F32 = jnp.float32


def angles(length, count, shift, rows=None):
    k = np.arange(length if rows is None else rows)[:, None]
    m = np.arange(count)[None, :] - shift
    phase = np.mod(k * m, length).astype(np.float64) * (2.0 * math.pi / length)
    return np.cos(phase), np.sin(phase)


def pad_to(a, rows, cols):
    return np.pad(a, ((0, rows - a.shape[0]), (0, cols - a.shape[1])))


def tables(depth, slab, window):
    half = depth // 2 + 1
    c, s = angles(window, window, 0)
    fx = np.block([[c, -s], [s, c]])
    fy = np.block([[c, s], [-s, c]])
    iy = np.block([[c, -s], [s, c]])
    ix = np.concatenate([c, -s], 0)
    cz, sz = angles(depth, depth, 0, half)
    fz = np.concatenate([pad_to(cz, KP, depth), pad_to(-sz, KP, depth)], 0)
    ct, st = angles(depth, TMPL, HALF, half)
    tz = np.concatenate([pad_to(ct, TMPL, TMPL), pad_to(st, TMPL, TMPL)], 0)
    cw, sw = angles(window, TMPL, HALF)
    cp, sp = pad_to(cw.T, CUBE, window), pad_to(sw.T, CUBE, window)
    zero = np.zeros_like(cp)
    tx = np.block(
        [[cp, sp, zero, zero], [zero, zero, cp, sp], [-sp, cp, zero, zero], [zero, zero, -sp, cp]]
    )
    ty = np.block([[cw, -sw], [sw, cw]])
    weight = np.full((half,), 2.0)
    weight[0] = 1.0
    if depth % 2 == 0:
        weight[-1] = 1.0
    cq = np.round(cz[:, HALF : HALF + slab].T, 12) * weight
    sq = np.round(sz[:, HALF : HALF + slab].T, 12) * weight
    cq, sq = pad_to(cq, slab, KP), pad_to(sq, slab, KP)
    iz = np.block([[cq, -sq], [sq, cq]])
    gap = np.arange(depth)[None, :] - np.arange(slab)[:, None]
    bz = ((gap >= 0) & (gap < TMPL)).astype(np.float64)
    bz = np.concatenate([bz, bz], 1)
    turn = np.mod(np.arange(window)[:, None] - np.arange(window)[None, :] + HALF, window)
    bx = (turn < TMPL).astype(np.float64)
    bx = np.concatenate([bx, bx], 0)
    return [jnp.asarray(t, BF16) for t in (fx, fy, iy, ix, fz, tz, tx, ty, iz, bz, bx)]


def dot(a, b):
    return jnp.dot(a, b, preferred_element_type=F32)


def split(a):
    high = a.astype(BF16)
    return high, (a - high.astype(F32)).astype(BF16)


def correlate(
    bands, slab, depth, window,
    x_ref, t_ref, fx, fy, iy, ix, fz, tz, tx, ty, iz, bz, bx,
    corr_ref, inv_ref,
    stage, spec, cube, wide, lines, rows_e,
):
    pairs = (depth // 2 + 2) // 2
    band_rows = window // bands
    count = t_ref.shape[0]
    me = lax.axis_index("rot")

    @pl.loop(0, window // 2)
    def _(i):
        both = jnp.concatenate([x_ref[2 * i], x_ref[2 * i + 1]], axis=1)
        out = dot(fz[...], both)
        stage[pl.ds(2 * i, 2 * KP, stride=window), :] = out[:, :window]
        stage[pl.ds(2 * i + 1, 2 * KP, stride=window), :] = out[:, window:]

    @pl.loop(0, pairs)
    def _(i):
        def plane(k):
            return stage[pl.ds(pl.multiple_of(k * window, window), window), :]

        top = jnp.concatenate([plane(2 * i), plane(KP + 2 * i)], axis=1)
        low = jnp.concatenate([plane(2 * i + 1), plane(KP + 2 * i + 1)], axis=1)
        out = dot(jnp.concatenate([top, low], axis=0).astype(BF16), fx[...]).astype(BF16)
        left = jnp.concatenate([out[:window, :window], out[:window, window:]], axis=0)
        right = jnp.concatenate([out[window:, :window], out[window:, window:]], axis=0)
        spec[i] = dot(fy[...], jnp.concatenate([left, right], axis=1)).astype(BF16)

    reach = band_rows + TMPL - 1

    @pl.loop(0, reach)
    def _(j):
        row = lax.rem(me * band_rows + j + window - HALF, window)
        value = x_ref[row].astype(F32)
        high, low = split(value * value)
        rows_e[j] = dot(bz[...], jnp.concatenate([high, low], axis=0))

    sums = rows_e[...]
    for step in (1, 2, 4, 8):
        sums = sums[: sums.shape[0] - step] + sums[step:]
    total = sums[:band_rows] + sums[16 : 16 + band_rows] + sums[32 : 32 + band_rows]
    high, low = split(total.reshape(band_rows * slab, window))
    energy = dot(jnp.concatenate([high, low], axis=1), bx[...])
    inv_ref[...] = 1.0 / (depth * window * window * jnp.sqrt(energy / TMPL**3 + 1e-05))

    lines[...] = jnp.zeros_like(lines)
    for r in range(count):
        chunks = TMPL * CUBE // window
        for c in range(chunks):
            out = dot(tz[...], t_ref[r, :, c * window : (c + 1) * window]).astype(BF16)
            cube[c * TMPL : (c + 1) * TMPL, :window] = out[:TMPL]
            cube[c * TMPL : (c + 1) * TMPL, window:] = out[TMPL:]
        for c in range(chunks):
            out = dot(cube[c * TMPL : (c + 1) * TMPL, :], tx[...])
            for e in range(2):
                for p in range(2):
                    at = (2 * e + p) * window
                    wide[pl.ds(p * TMPL + 2 * c + e, KP, stride=2 * TMPL), :] = out[
                        :KP, at : at + window
                    ]

        @pl.loop(0, pairs)
        def _(i):
            at = pl.multiple_of(i * (4 * TMPL), 4 * TMPL)
            rhs = jnp.concatenate(
                [wide[pl.ds(at, 2 * TMPL), :], wide[pl.ds(at + 2 * TMPL, 2 * TMPL), :]], axis=1
            ).astype(BF16)
            temp = dot(ty[...], rhs).astype(BF16).astype(F32)
            freq = spec[i].astype(F32)
            tr, ti = temp[:window], temp[window:]
            sr, si = freq[:window], freq[window:]
            prod = jnp.concatenate([sr * tr - si * ti, sr * ti + si * tr], axis=0).astype(BF16)
            out = dot(iy[...], prod)
            for e in range(2):
                for p in range(2):
                    lines[pl.ds(p * KP + 2 * i + e, window, stride=2 * KP), :] = out[
                        p * window : (p + 1) * window, e * window : (e + 1) * window
                    ]

        @pl.loop(0, bands)
        def _(b):
            parts = []
            for j in range(band_rows // 2):
                at = pl.multiple_of((b * band_rows + 2 * j) * (2 * KP), 4 * KP)
                rhs = jnp.concatenate(
                    [lines[pl.ds(at, 2 * KP), :], lines[pl.ds(at + 2 * KP, 2 * KP), :]], axis=1
                ).astype(BF16)
                out = dot(iz[...], rhs)
                for e in range(2):
                    one = out[:, e * window : (e + 1) * window]
                    parts.append(jnp.concatenate([one[:slab], one[slab:]], axis=1))
            corr_ref[b, r] = dot(jnp.concatenate(parts, axis=0).astype(BF16), ix[...]).astype(BF16)


def combine(bands, count, corr_ref, inv_ref, fac_ref, best_ref, orient_ref, got, facs,
            send, recv, send_f, recv_f):
    me = lax.axis_index("rot")
    barrier = pltpu.get_barrier_semaphore()
    for d in range(1, bands):
        peer = lax.rem(me + d, bands)
        pl.semaphore_signal(
            barrier, inc=1, device_id={"rot": peer}, device_id_type=pl.DeviceIdType.MESH
        )
    pl.semaphore_wait(barrier, bands - 1)
    copies = []
    for d in range(1, bands):
        peer = lax.rem(me + d, bands)
        for src, dst, s, t in (
            (fac_ref, facs.at[d], send_f.at[d], recv_f.at[d]),
            (corr_ref.at[peer], got.at[d], send.at[d], recv.at[d]),
        ):
            copy = pltpu.make_async_remote_copy(
                src_ref=src, dst_ref=dst, send_sem=s, recv_sem=t,
                device_id={"rot": peer}, device_id_type=pl.DeviceIdType.MESH,
            )
            copy.start()
            copies.append(copy)
    got[0] = corr_ref[me]
    facs[0] = fac_ref[...]
    for copy in copies:
        copy.wait()
    rows = inv_ref.shape[0]
    step = 32

    @pl.loop(0, rows // step)
    def _(i):
        at = pl.ds(pl.multiple_of(i * step, step), step)
        inv = inv_ref[at, :]
        best = None
        for d in range(bands):
            for r in range(count):
                value = got[d, r, at, :].astype(F32) * inv
                best = value if best is None else jnp.maximum(best, value)
        total = jnp.zeros_like(best)
        moment = jnp.zeros_like(best)
        for d in range(bands):
            for r in range(count):
                value = got[d, r, at, :].astype(F32) * inv
                weight = jnp.square(jnp.maximum(value - best + 1.0, 0.0))
                total = total + weight
                moment = moment + weight * facs[d, r : r + 1, :]
        best_ref[at, :] = best
        orient_ref[at, :] = moment / total


VMEM = pl.BlockSpec(memory_space=pltpu.VMEM)


def on_device(tomogram, templates, rotation_ids):
    slab, window = tomogram.shape[0], tomogram.shape[1]
    count = templates.shape[0]
    depth = slab + TMPL
    bands, slabs = lax.axis_size("rot"), lax.axis_size("slab")
    band_rows = window // bands
    turned = jnp.swapaxes(tomogram, 0, 1)
    up = [(i, i + 1) for i in range(slabs - 1)]
    down = [(j, i) for i, j in up]
    before = lax.ppermute(turned[:, slab - HALF :], "slab", up)
    after = lax.ppermute(turned[:, :HALF], "slab", down)
    padded = jnp.concatenate([before, turned, after], axis=1)
    cubes = jnp.pad(
        templates.reshape(count, TMPL, TMPL, TMPL), ((0, 0), (0, 0), (0, 0), (0, CUBE - TMPL))
    ).reshape(count, TMPL, TMPL * CUBE)
    pairs = (depth // 2 + 2) // 2
    corr, inv = pl.pallas_call(
        functools.partial(correlate, bands, slab, depth, window),
        out_shape=(
            jax.ShapeDtypeStruct((bands, count, band_rows * slab, window), BF16),
            jax.ShapeDtypeStruct((band_rows * slab, window), F32),
        ),
        in_specs=[VMEM] * 13,
        out_specs=(VMEM, VMEM),
        scratch_shapes=[
            pltpu.VMEM((2 * KP * window, window), F32),
            pltpu.VMEM((pairs, 2 * window, 2 * window), BF16),
            pltpu.VMEM((TMPL * CUBE // window * TMPL, 2 * window), BF16),
            pltpu.VMEM((KP * 2 * TMPL, window), F32),
            pltpu.VMEM((window * 2 * KP, window), F32),
            pltpu.VMEM((band_rows + TMPL - 1, slab, window), F32),
        ],
        compiler_params=pltpu.CompilerParams(vmem_limit_bytes=50 * 2**20),
        name="correlate",
    )(padded, cubes, *tables(depth, slab, window))
    factors = 1.0 - (2.0 * rotation_ids.astype(F32) + 1.0) / (count * bands)
    factors = jnp.broadcast_to(
        jnp.pad(factors, (0, 8 * pl.cdiv(count, 8) - count))[:, None],
        (8 * pl.cdiv(count, 8), window),
    )
    sems = [pltpu.SemaphoreType.DMA((bands,))] * 4
    best, orient = pl.pallas_call(
        functools.partial(combine, bands, count),
        out_shape=(jax.ShapeDtypeStruct(inv.shape, F32), jax.ShapeDtypeStruct(inv.shape, F32)),
        in_specs=[VMEM] * 3,
        out_specs=(VMEM, VMEM),
        scratch_shapes=[
            pltpu.VMEM((bands,) + corr.shape[1:], BF16),
            pltpu.VMEM((bands,) + factors.shape, F32),
        ]
        + sems,
        compiler_params=pltpu.CompilerParams(
            collective_id=0, has_side_effects=True, vmem_limit_bytes=32 * 2**20
        ),
        name="combine",
    )(corr, inv, factors)

    def placed(a):
        return jnp.swapaxes(a.reshape(band_rows, slab, window), 0, 1)

    return placed(best), placed(orient)


def solution(mesh):
    return jax.shard_map(
        on_device,
        mesh=mesh,
        in_specs=(P("slab", None, None), P("rot", None, None), P("rot")),
        out_specs=(P("slab", "rot", None), P("slab", "rot", None)),
        check_vma=False,
    )
```

time: 392 us -> 114 us (0.29); the launches traced: 386 us -> 114 us
  waiting for transfers between devices: 202 us -> 7.83 us
  Pallas kernels: 0 us -> 89.1 us
  matrix products: 70.7 us -> 0 us
  local copies, waits for them, and re-layouts: 44.2 us -> 7.18 us
  other arithmetic: 31.1 us -> 3.28 us
  loops' own time: 17.9 us -> 0 us
  between operations: 14 us -> 0.85 us
    reduce_scatter x2 -> x0, waiting for transfers between devices: 126 us -> none  [the longest x1 65.4 us: on_device(): lax.psum_scatter(weight_total.astype(jnp.bfloat16), 'rot', scatter_dimens...]
    pallas_call x0 -> x2, Pallas kernels: none -> 89.1 us  [the longest x1 56.8 us: on_device(): pl.pallas_call(functools.partial(correlate, bands, slab, depth, window),...]
    pmax x1 -> x0, waiting for transfers between devices: 72.5 us -> none  [on_device(): lax.pmax(local_best.astype(jnp.bfloat16), 'rot').astype(local_best.dtype)]
    dot_general x38 -> x0, matrix products: 70.7 us -> none  [the longest x35 60.8 us: product_of(): return jnp.einsum(form, left, right, preferred_element_type=jnp.float32)]
    while x33 -> x0, local copies, waits for them, and re-layouts: 20.9 us -> none  [the longest x1 12.3 us: on_device(): spectrum = lax.map(column_step, jnp.arange(row_groups, dtype=jnp.int32))]
    another operation x5 -> x0, loops' own time: 17.9 us -> none  [the longest x2 15.4 us: one_rotation(): inverse_parts = lax.map(row_step, jnp.arange(row_groups, dtype=jnp.int32))]
    another operation x31 -> x0, other arithmetic: 16.7 us -> none
    dynamic_slice x15 -> x0, local copies, waits for them, and re-layouts: 10.6 us -> none  [the longest x12 7.07 us: on_device(): spectrum = lax.map(column_step, jnp.arange(row_groups, dtype=jnp.int32))]
  transfers between devices with their start and end apart: 5 -> 2, of which waited for: 4 -> 2; matrix products, arithmetic and copies ran while one was open for 3% -> 3% of each run, Pallas kernels for 0% -> 0%
where the time goes in v1:
time: 114 us
  Pallas kernels  89.1 us (78%)
  waiting for transfers between devices  7.83 us (7%)
  local copies, waits for them, and re-layouts  7.18 us (6%)
  starting transfers between devices  5.59 us (5%)
  other arithmetic  3.28 us (3%)
    pallas_call x1, Pallas kernels, on_device(): pl.pallas_call(functools.partial(correlate, bands, slab, depth, window),...  56.8 us
    pallas_call x1, Pallas kernels, on_device(): pl.pallas_call(functools.partial(combine, bands, count), out_shape=(jax.S...  32.3 us
    ppermute x1, waiting for transfers between devices, on_device(): after = lax.ppermute(turned[:, :HALF], 'slab', down)  4.4 us
    ppermute x1, starting transfers between devices, on_device(): before = lax.ppermute(turned[:, slab - HALF:], 'slab', up)  3.67 us
    ppermute x1, waiting for transfers between devices, on_device(): before = lax.ppermute(turned[:, slab - HALF:], 'slab', up)  3.43 us
    concatenate x1, other arithmetic, on_device(): padded = jnp.concatenate([before, turned, after], axis=1)  3.27 us
    reshape x1, local copies, waits for them, and re-layouts, on_device(): templates.reshape(count, TMPL, TMPL, TMPL)  2.66 us
    unnamed x23, local copies, waits for them, and re-layouts  2.61 us
  transfers between devices with their start and end apart: 2, of which 2 were waited for; matrix products, arithmetic and copies ran while one was open for 3% of the time, Pallas kernels for 0%

profile of v1, /device:TPU:13, one launch (start us, length us, event | category | flops | bytes accessed | tf_op | source)
XLA Modules:
  0.0 113.8 jit_solution(3522456139342693089)
XLA Ops:
  0.6 2.5 %copy.22 = bf16[24,128,128]{2,0,1:T(8,128)(2,1)} copy(bf16[24,128,128]{2,1,0:T(8,128)(2,1)} %param.14) | data formatting | bytes 1572864 | tf_op args[0]
  3.2 3.7 %collective-permute-start = (bf16[128,24,128]{2,1,0:T(8,128)(2,1)}, bf16[128,24,128]{2,1,0:T(8,128)(2,1)}, u32[]{:S(2)}, u32[]{:S(2)}) collective-permute-start(bf16[128,24,128]{2,1,0:T(8,128)(2,1)} %bitcast.10), channel_id=1, source_target_pairs={{0,8},{8,16},{16,24},{1,9},{9,17},{17,25},{2,10},{10,18},{18,26},{... | collective-permute-start | bytes 2359304 | tf_op jit(solution)/shard_map/ppermute | solution.py:234
  6.8 1.9 %collective-permute-start.1 = (bf16[128,24,128]{2,1,0:T(8,128)(2,1)}, bf16[128,24,128]{2,1,0:T(8,128)(2,1)}, u32[]{:S(2)}, u32[]{:S(2)}) collective-permute-start(bf16[128,24,128]{2,1,0:T(8,128)(2,1)} %bitcast.10), channel_id=1, source_target_pairs={{8,0},{16,8},{24,16},{9,1},{17,9},{25,17},{10,2},{18,10},{26,18},{... | collective-permute-start | bytes 2359304 | tf_op jit(solution)/shard_map/ppermute | solution.py:235
  8.8 2.7 %reshape.17 = bf16[2,48,48,48]{3,2,1,0:T(8,128)(2,1)S(1)} reshape(bf16[2,48,2304]{2,1,0:T(8,128)(2,1)} %param.15) | data formatting | bytes 884736 | tf_op jit(solution)/shard_map/reshape | solution.py:238
  11.4 0.0 copy-start.10
  11.4 0.2 pad.8
  11.7 0.8 reshape.18.t_ref
  12.5 0.0 copy-done.10
  12.5 0.0 copy-start
  12.5 0.0 copy-start.1
  12.5 0.0 copy-start.2
  12.6 0.0 copy-start.3
  12.6 0.0 copy-start.4
  12.6 0.0 copy-start.5
  12.6 0.0 copy-start.6
  12.6 0.0 copy-start.7
  12.6 0.0 copy-start.8
  12.6 0.0 copy-start.9
  12.6 3.4 %collective-permute-done = bf16[128,24,128]{2,1,0:T(8,128)(2,1)} collective-permute-done((bf16[128,24,128]{2,1,0:T(8,128)(2,1)}, bf16[128,24,128]{2,1,0:T(8,128)(2,1)}, u32[]{:S(2)}, u32[]{:S(2)}) %collective-permute-start) | collective-permute-done | bytes 786464 | tf_op jit(solution)/shard_map/ppermute | solution.py:234
  16.1 4.4 %collective-permute-done.1 = bf16[128,24,128]{2,1,0:T(8,128)(2,1)} collective-permute-done((bf16[128,24,128]{2,1,0:T(8,128)(2,1)}, bf16[128,24,128]{2,1,0:T(8,128)(2,1)}, u32[]{:S(2)}, u32[]{:S(2)}) %collective-permute-start.1) | collective-permute-done | bytes 786464 | tf_op jit(solution)/shard_map/ppermute | solution.py:235
  20.5 3.3 %pad_maximum_fusion.x_ref = bf16[128,72,128]{2,1,0:T(8,128)(2,1)} fusion(bf16[128,24,128]{2,1,0:T(8,128)(2,1)} %collective-permute-done.1, bf16[128,24,128]{2,1,0:T(8,128)(2,1)} %bitcast.10, bf16[128,24,128]{2,1,0:T(8,128)(2,1)} %collective-permute-done), kind=kLoop, calls=%fused_computation | loop fusion | flops 7077888 | bytes 4718592 | tf_op jit(solution)/shard_map/concatenate | solution.py:236
  23.7 0.0 copy-done
  23.7 0.0 copy-done.1
  23.7 0.0 copy-done.2
  23.7 0.0 copy-done.3
  23.8 0.0 copy-done.4
  23.8 0.0 copy-done.5
  23.8 0.0 copy-done.6
  23.8 56.8 %correlate.1 = (bf16[8,2,384,128]{3,2,1,0:T(8,128)(2,1)S(1)}, f32[384,128]{1,0:T(8,128)S(1)}) custom-call(bf16[128,72,128]{2,1,0:T(8,128)(2,1)} %pad_maximum_fusion.x_ref, bf16[2,48,3072]{2,1,0:T(8,128)(2,1)S(1)} %reshape.18.t_ref, bf16[256,256]{1,0:T(8,128)(2,1)S(1)} %copy-done, bf16[256,256]{1,0:T(8,128)(2,1)S(1)} %copy-done.2, ...), custom_call_target="tpu_custom_call" | custom-call | tf_op jit(solution)/shard_map/correlate/pallas_call | solution.py:241
  80.6 0.1 broadcast_in_dim.2.fac_ref
  80.7 32.3 %combine.1 = (f32[384,128]{1,0:T(8,128)S(1)}, f32[384,128]{1,0:T(8,128)S(1)}) custom-call(bf16[8,2,384,128]{3,2,1,0:T(8,128)(2,1)S(1)} %get-tuple-element.6.corr_ref, f32[384,128]{1,0:T(8,128)S(1)} %get-tuple-element.7.inv_ref, f32[8,128]{1,0:T(8,128)S(1)} %broadcast_in_dim.2.fac_ref), custom_call_target="tpu_custom_call" | custom-call | tf_op jit(solution)/shard_map/combine/pallas_call | solution.py:266
  113.0 0.8 copy_bitcast_fusion.1
  (5 shorter events, 0.0 us)
Async XLA Ops:
  3.2 12.9 %collective-permute-start = (bf16[128,24,128]{2,1,0:T(8,128)(2,1)}, bf16[128,24,128]{2,1,0:T(8,128)(2,1)}, u32[]{:S(2)}, u32[]{:S(2)}) collective-permute-start(bf16[128,24,128]{2,1,0:T(8,128)(2,1)} %bitcast.10), channel_id=1, source_target_pairs={{0,8},{8,16},{16,24},{1,9},{9,17},{17,25},{2,10},{10,18},{18,26},{... | collective-permute-start | bytes 2359304 | tf_op jit(solution)/shard_map/ppermute | solution.py:234
  6.8 13.6 %collective-permute-start.1 = (bf16[128,24,128]{2,1,0:T(8,128)(2,1)}, bf16[128,24,128]{2,1,0:T(8,128)(2,1)}, u32[]{:S(2)}, u32[]{:S(2)}) collective-permute-start(bf16[128,24,128]{2,1,0:T(8,128)(2,1)} %bitcast.10), channel_id=1, source_target_pairs={{8,0},{16,8},{24,16},{9,1},{17,9},{25,17},{10,2},{18,10},{26,18},{... | collective-permute-start | bytes 2359304 | tf_op jit(solution)/shard_map/ppermute | solution.py:235
  11.4 1.0 copy-start.10
  12.5 11.2 %copy-start = (bf16[256,256]{1,0:T(8,128)(2,1)S(1)}, bf16[256,256]{1,0:T(8,128)(2,1)}, u32[]{:S(2)}) copy-start(bf16[256,256]{1,0:T(8,128)(2,1)} %constant.32.clone.fx.iy) | copy-start | bytes 393220
  12.5 11.2 %copy-start.1 = (bf16[256,512]{1,0:T(8,128)(2,1)S(1)}, bf16[256,512]{1,0:T(8,128)(2,1)}, u32[]{:S(2)}) copy-start(bf16[256,512]{1,0:T(8,128)(2,1)} %constant.37.clone.tx) | copy-start | bytes 786436
  12.5 11.2 %copy-start.2 = (bf16[256,256]{1,0:T(8,128)(2,1)S(1)}, bf16[256,256]{1,0:T(8,128)(2,1)}, u32[]{:S(2)}) copy-start(bf16[256,256]{1,0:T(8,128)(2,1)} %constant.33.clone.fy) | copy-start | bytes 393220
  12.6 11.2 %copy-start.3 = (bf16[256,128]{1,0:T(8,128)(2,1)S(1)}, bf16[256,128]{1,0:T(8,128)(2,1)}, u32[]{:S(2)}) copy-start(bf16[256,128]{1,0:T(8,128)(2,1)} %constant.34.clone.ix) | copy-start | bytes 196612
  12.6 11.2 %copy-start.4 = (bf16[256,96]{1,0:T(8,128)(2,1)S(1)}, bf16[256,96]{1,0:T(8,128)(2,1)}, u32[]{:S(2)}) copy-start(bf16[256,96]{1,0:T(8,128)(2,1)} %constant.38.clone.ty) | copy-start | bytes 147460
  12.6 11.2 %copy-start.5 = (bf16[256,128]{1,0:T(8,128)(2,1)S(1)}, bf16[256,128]{1,0:T(8,128)(2,1)}, u32[]{:S(2)}) copy-start(bf16[256,128]{1,0:T(8,128)(2,1)} %constant.41.clone.bx) | copy-start | bytes 196612
  12.6 11.2 %copy-start.6 = (bf16[96,48]{1,0:T(8,128)(2,1)S(1)}, bf16[96,48]{1,0:T(8,128)(2,1)}, u32[]{:S(2)}) copy-start(bf16[96,48]{1,0:T(8,128)(2,1)} %constant.36.clone.tz) | copy-start | bytes 27652
  12.6 11.2 %copy-start.7 = (bf16[80,72]{1,0:T(8,128)(2,1)S(1)}, bf16[80,72]{1,0:T(8,128)(2,1)}, u32[]{:S(2)}) copy-start(bf16[80,72]{1,0:T(8,128)(2,1)} %constant.35.clone.fz) | copy-start | bytes 34564
  12.6 11.2 %copy-start.8 = (bf16[48,80]{1,0:T(8,128)(2,1)S(1)}, bf16[48,80]{1,0:T(8,128)(2,1)}, u32[]{:S(2)}) copy-start(bf16[48,80]{1,0:T(8,128)(2,1)} %constant.39.clone.iz) | copy-start | bytes 23044
  12.6 11.2 %copy-start.9 = (bf16[24,144]{1,0:T(8,128)(2,1)S(1)}, bf16[24,144]{1,0:T(8,128)(2,1)}, u32[]{:S(2)}) copy-start(bf16[24,144]{1,0:T(8,128)(2,1)} %constant.40.clone.bz) | copy-start | bytes 20740

commit v2 on v1

v2 whole, which is shorter than its diff:
```python
import functools
import math

import jax
import jax.numpy as jnp
import numpy as np
from jax import lax
from jax.experimental import pallas as pl
from jax.experimental.pallas import tpu as pltpu
from jax.sharding import PartitionSpec as P

TMPL = 48
HALF = TMPL // 2
KP = 40
CUBE = 64
BF16 = jnp.bfloat16
F32 = jnp.float32


def angles(length, count, shift, rows=None):
    k = np.arange(length if rows is None else rows)[:, None]
    m = np.arange(count)[None, :] - shift
    phase = np.mod(k * m, length).astype(np.float64) * (2.0 * math.pi / length)
    return np.cos(phase), np.sin(phase)


def pad_to(a, rows, cols):
    return np.pad(a, ((0, rows - a.shape[0]), (0, cols - a.shape[1])))


def tables(depth, slab, window):
    half = depth // 2 + 1
    c, s = angles(window, window, 0)
    fx = np.block([[c, -s], [s, c]])
    fy = np.block([[c, s], [-s, c]])
    iy = np.block([[c, -s], [s, c]])
    ix = np.concatenate([c, -s], 0)
    cz, sz = angles(depth, depth, 0, half)
    fz = np.concatenate([pad_to(cz, KP, depth), pad_to(-sz, KP, depth)], 0)
    ct, st = angles(depth, TMPL, HALF, half)
    tz = np.concatenate([pad_to(ct, TMPL, TMPL), pad_to(st, TMPL, TMPL)], 0)
    cw, sw = angles(window, TMPL, HALF)
    cp, sp = pad_to(cw.T, CUBE, window), pad_to(sw.T, CUBE, window)
    zero = np.zeros_like(cp)
    tx = np.block(
        [[cp, sp, zero, zero], [zero, zero, cp, sp], [-sp, cp, zero, zero], [zero, zero, -sp, cp]]
    )
    ty = np.block([[cw, -sw], [sw, cw]])
    weight = np.full((half,), 2.0)
    weight[0] = 1.0
    if depth % 2 == 0:
        weight[-1] = 1.0
    cq = np.round(cz[:, HALF : HALF + slab].T, 12) * weight
    sq = np.round(sz[:, HALF : HALF + slab].T, 12) * weight
    cq, sq = pad_to(cq, slab, KP), pad_to(sq, slab, KP)
    iz = np.block([[cq, -sq], [sq, cq]])
    gap = np.arange(depth)[None, :] - np.arange(slab)[:, None]
    bz = ((gap >= 0) & (gap < TMPL)).astype(np.float64)
    bz = np.concatenate([bz, bz], 1)
    turn = np.mod(np.arange(window)[:, None] - np.arange(window)[None, :] + HALF, window)
    bx = (turn < TMPL).astype(np.float64)
    bx = np.concatenate([bx, bx], 0)
    return [jnp.asarray(t, BF16) for t in (fx, fy, iy, ix, fz, tz, tx, ty, iz, bz, bx)]


def dot(a, b):
    return jnp.dot(a, b, preferred_element_type=F32)


def split(a):
    high = a.astype(BF16)
    return high, (a - high.astype(F32)).astype(BF16)


def cast_rows(ref, at, size):
    return ref[pl.ds(pl.multiple_of(at, 8), size), :]


def correlate(
    bands, slabs, slab, depth, window,
    tom, t_ref, fac_ref, fx, fy, iy, ix, fz, tz, tx, ty, iz, bz, bx,
    best_ref, orient_ref,
    halo, block, stage, spec, cube, wide, lines, rows_e, inv_ref, corr, got, facs,
    halo_send, halo_recv, send, recv, send_f, recv_f,
):
    pairs = KP // 2
    band_rows = window // bands
    count = t_ref.shape[0]
    me = lax.axis_index("rot")
    at_slab = lax.axis_index("slab")
    has_left, has_right = at_slab > 0, at_slab < slabs - 1
    mesh_ids = pl.DeviceIdType.MESH

    barrier = pltpu.get_barrier_semaphore()
    for d in range(1, bands):
        peer = lax.rem(me + d, bands)
        pl.semaphore_signal(barrier, inc=1, device_id={"rot": peer}, device_id_type=mesh_ids)

    @pl.when(has_left)
    def _():
        pl.semaphore_signal(
            barrier, inc=1, device_id={"slab": at_slab - 1}, device_id_type=mesh_ids
        )

    @pl.when(has_right)
    def _():
        pl.semaphore_signal(
            barrier, inc=1, device_id={"slab": at_slab + 1}, device_id_type=mesh_ids
        )

    around = has_left.astype(jnp.int32) + has_right.astype(jnp.int32)
    pl.semaphore_wait(barrier, bands - 1 + around)

    def to_right():
        return pltpu.make_async_remote_copy(
            src_ref=tom.at[pl.ds(slab - HALF, HALF)], dst_ref=halo.at[0],
            send_sem=halo_send.at[0], recv_sem=halo_recv.at[0],
            device_id={"slab": at_slab + 1}, device_id_type=mesh_ids,
        )

    def to_left():
        return pltpu.make_async_remote_copy(
            src_ref=tom.at[pl.ds(0, HALF)], dst_ref=halo.at[1],
            send_sem=halo_send.at[1], recv_sem=halo_recv.at[1],
            device_id={"slab": at_slab - 1}, device_id_type=mesh_ids,
        )

    def factor_copy(d):
        return pltpu.make_async_remote_copy(
            src_ref=fac_ref, dst_ref=facs.at[d], send_sem=send_f.at[d], recv_sem=recv_f.at[d],
            device_id={"rot": lax.rem(me + d, bands)}, device_id_type=mesh_ids,
        )

    def score_copy(d, r):
        peer = lax.rem(me + d, bands)
        return pltpu.make_async_remote_copy(
            src_ref=corr.at[peer, r], dst_ref=got.at[d, r],
            send_sem=send.at[r, d], recv_sem=recv.at[r, d],
            device_id={"rot": peer}, device_id_type=mesh_ids,
        )

    @pl.when(has_right)
    def _():
        to_right().start()

    @pl.when(has_left)
    def _():
        to_left().start()

    for d in range(1, bands):
        factor_copy(d).start()
    facs[0] = fac_ref[...]

    chunks = TMPL * CUBE // window
    for r in range(count):
        for c in range(chunks):
            out = dot(tz[...], t_ref[r, :, c * window : (c + 1) * window]).astype(BF16)
            cube[c * TMPL : (c + 1) * TMPL, :window] = out[:TMPL]
            cube[c * TMPL : (c + 1) * TMPL, window:] = out[TMPL:]
        for c in range(chunks):
            out = dot(cube[c * TMPL : (c + 1) * TMPL, :], tx[...])
            for e in range(2):
                for p in range(2):
                    at = (2 * e + p) * window
                    wide[r, pl.ds(p * TMPL + 2 * c + e, KP, stride=2 * TMPL), :] = out[
                        :KP, at : at + window
                    ]

    @pl.loop(0, slab)
    def _(z):
        block[pl.ds(HALF + z, window, stride=depth), :] = tom[z].astype(F32)

    @pl.when(has_left)
    def _():
        to_left().wait_send()

    @pl.when(has_right)
    def _():
        to_right().wait_send()

    @pl.when(has_left)
    def _():
        to_right().wait_recv()

    @pl.when(has_right)
    def _():
        to_left().wait_recv()

    for side, there, first in ((0, has_left, 0), (1, has_right, HALF + slab)):
        @pl.when(there)
        def _():
            @pl.loop(0, HALF)
            def _(z):
                block[pl.ds(first + z, window, stride=depth), :] = halo[side, z].astype(F32)

        @pl.when(jnp.logical_not(there))
        def _():
            @pl.loop(0, HALF)
            def _(z):
                block[pl.ds(first + z, window, stride=depth), :] = jnp.zeros((window, window), F32)

    group = 8

    @pl.loop(0, window // group)
    def _(i):
        y = i * group
        several = jnp.concatenate(
            [cast_rows(block, (y + j) * depth, depth) for j in range(group)], axis=1
        )
        out = dot(fz[...], several.astype(BF16))
        for j in range(group):
            stage[pl.ds(y + j, 2 * KP, stride=window), :] = out[:, j * window : (j + 1) * window]

    @pl.loop(0, pairs, unroll=4)
    def _(i):
        def plane(k):
            return cast_rows(stage, k * window, window)

        top = jnp.concatenate([plane(2 * i), plane(KP + 2 * i)], axis=1)
        low = jnp.concatenate([plane(2 * i + 1), plane(KP + 2 * i + 1)], axis=1)
        out = dot(jnp.concatenate([top, low], axis=0).astype(BF16), fx[...]).astype(BF16)
        left = jnp.concatenate([out[:window, :window], out[:window, window:]], axis=0)
        right = jnp.concatenate([out[window:, :window], out[window:, window:]], axis=0)
        spec[i] = dot(fy[...], jnp.concatenate([left, right], axis=1)).astype(BF16)

    for r in range(count):
        @pl.loop(0, pairs, unroll=2)
        def _(i):
            at = pl.multiple_of(i * (4 * TMPL), 4 * TMPL)
            rhs = jnp.concatenate(
                [wide[r, pl.ds(at, 2 * TMPL), :], wide[r, pl.ds(at + 2 * TMPL, 2 * TMPL), :]],
                axis=1,
            ).astype(BF16)
            temp = dot(ty[...], rhs).astype(BF16).astype(F32)
            freq = spec[i].astype(F32)
            tr, ti = temp[:window], temp[window:]
            sr, si = freq[:window], freq[window:]
            prod = jnp.concatenate([sr * tr - si * ti, sr * ti + si * tr], axis=0).astype(BF16)
            out = dot(iy[...], prod)
            for e in range(2):
                for p in range(2):
                    lines[pl.ds(p * KP + 2 * i + e, window, stride=2 * KP), :] = out[
                        p * window : (p + 1) * window, e * window : (e + 1) * window
                    ]

        @pl.loop(1, bands + 1)
        def _(d):
            b = lax.rem(me + d, bands)
            parts = []
            for j in range(band_rows // 2):
                at = (b * band_rows + 2 * j) * (2 * KP)
                rhs = jnp.concatenate(
                    [cast_rows(lines, at, 2 * KP), cast_rows(lines, at + 2 * KP, 2 * KP)], axis=1
                ).astype(BF16)
                out = dot(iz[...], rhs)
                for e in range(2):
                    one = out[:, e * window : (e + 1) * window]
                    parts.append(jnp.concatenate([one[:slab], one[slab:]], axis=1))
            corr[b, r] = dot(jnp.concatenate(parts, axis=0).astype(BF16), ix[...]).astype(BF16)

            @pl.when(d < bands)
            def _():
                score_copy(d, r).start()

    got[0] = corr[me]

    reach = band_rows + TMPL - 1

    together = max(g for g in range(1, 10) if reach % g == 0)

    @pl.loop(0, reach // together)
    def _(i):
        first = i * together
        parts = []
        for j in range(together):
            row = lax.rem(me * band_rows + first + j + window - HALF, window)
            value = cast_rows(block, row * depth, depth)
            parts.append(jnp.concatenate(split(value * value), axis=0))
        out = dot(bz[...], jnp.concatenate(parts, axis=1))
        for j in range(together):
            rows_e[first + j] = out[:, j * window : (j + 1) * window]

    sums = rows_e[...]
    for step in (1, 2, 4, 8):
        sums = sums[: sums.shape[0] - step] + sums[step:]
    total = sums[:band_rows] + sums[16 : 16 + band_rows] + sums[32 : 32 + band_rows]
    high, low = split(total.reshape(band_rows * slab, window))
    energy = dot(jnp.concatenate([high, low], axis=1), bx[...])
    inv_ref[...] = 1.0 / (depth * window * window * jnp.sqrt(energy / TMPL**3 + 1e-05))

    for d in range(1, bands):
        factor_copy(d).wait()
    for r in range(count):
        for d in range(1, bands):
            score_copy(d, r).wait()
    rows = inv_ref.shape[0]
    step = 32

    @pl.loop(0, rows // step)
    def _(i):
        at = pl.ds(pl.multiple_of(i * step, step), step)
        inv = inv_ref[at, :]
        best = None
        for d in range(bands):
            for r in range(count):
                value = got[d, r, at, :].astype(F32) * inv
                best = value if best is None else jnp.maximum(best, value)
        total = jnp.zeros_like(best)
        moment = jnp.zeros_like(best)
        for d in range(bands):
            for r in range(count):
                value = got[d, r, at, :].astype(F32) * inv
                weight = jnp.square(jnp.maximum(value - best + 1.0, 0.0))
                total = total + weight
                moment = moment + weight * facs[d, r : r + 1, :]
        best_ref[at, :] = best
        orient_ref[at, :] = moment / total


VMEM = pl.BlockSpec(memory_space=pltpu.VMEM)


def on_device(tomogram, templates, rotation_ids):
    slab, window = tomogram.shape[0], tomogram.shape[1]
    count = templates.shape[0]
    depth = slab + TMPL
    bands, slabs = lax.axis_size("rot"), lax.axis_size("slab")
    band_rows = window // bands
    cubes = jnp.pad(
        templates.reshape(count, TMPL, TMPL, TMPL), ((0, 0), (0, 0), (0, 0), (0, CUBE - TMPL))
    ).reshape(count, TMPL, TMPL * CUBE)
    pairs = KP // 2
    factors = 1.0 - (2.0 * rotation_ids.astype(F32) + 1.0) / (count * bands)
    fac_rows = 8 * pl.cdiv(count, 8)
    factors = jnp.broadcast_to(
        jnp.pad(factors, (0, fac_rows - count))[:, None], (fac_rows, window)
    )
    rows = band_rows * slab
    dma = pltpu.SemaphoreType.DMA
    best, orient = pl.pallas_call(
        functools.partial(correlate, bands, slabs, slab, depth, window),
        out_shape=(jax.ShapeDtypeStruct((rows, window), F32),) * 2,
        in_specs=[VMEM] * 14,
        out_specs=(VMEM, VMEM),
        scratch_shapes=[
            pltpu.VMEM((2, HALF, window, window), BF16),
            pltpu.VMEM((window * depth, window), F32),
            pltpu.VMEM((2 * KP * window, window), F32),
            pltpu.VMEM((pairs, 2 * window, 2 * window), BF16),
            pltpu.VMEM((TMPL * CUBE // window * TMPL, 2 * window), BF16),
            pltpu.VMEM((count, KP * 2 * TMPL, window), F32),
            pltpu.VMEM((window * 2 * KP, window), F32),
            pltpu.VMEM((band_rows + TMPL - 1, slab, window), F32),
            pltpu.VMEM((rows, window), F32),
            pltpu.VMEM((bands, count, rows, window), BF16),
            pltpu.VMEM((bands, count, rows, window), BF16),
            pltpu.VMEM((bands, fac_rows, window), F32),
            dma((2,)), dma((2,)),
            dma((count, bands)), dma((count, bands)),
            dma((bands,)), dma((bands,)),
        ],
        compiler_params=pltpu.CompilerParams(
            collective_id=0, has_side_effects=True, vmem_limit_bytes=50 * 2**20
        ),
        name="correlate",
    )(tomogram, cubes, factors, *tables(depth, slab, window))

    def placed(a):
        return jnp.swapaxes(a.reshape(band_rows, slab, window), 0, 1)

    return placed(best), placed(orient)


def solution(mesh):
    return jax.shard_map(
        on_device,
        mesh=mesh,
        in_specs=(P("slab", None, None), P("rot", None, None), P("rot")),
        out_specs=(P("slab", "rot", None), P("slab", "rot", None)),
        check_vma=False,
    )
```

time: 114 us -> 66.1 us (0.58)
  Pallas kernels: 89.1 us -> 60.3 us
  waiting for transfers between devices: 7.83 us -> 0 us
  starting transfers between devices: 5.59 us -> 0 us
  other arithmetic: 3.28 us -> 0.01 us
  local copies, waits for them, and re-layouts: 7.18 us -> 4.87 us
    pallas_call x2 -> x1, Pallas kernels: 89.1 us -> 60.3 us  [on_device(): pl.pallas_call(functools.partial(correlate, bands, slabs, slab, depth, wi...]
    ppermute x2 -> x0, waiting for transfers between devices: 7.83 us -> none  [the longest x1 4.4 us: on_device(): after = lax.ppermute(turned[:, :HALF], 'slab', down)]
    ppermute x2 -> x0, starting transfers between devices: 5.59 us -> none  [the longest x1 3.67 us: on_device(): before = lax.ppermute(turned[:, slab - HALF:], 'slab', up)]
    concatenate x1 -> x0, other arithmetic: 3.27 us -> none  [on_device(): padded = jnp.concatenate([before, turned, after], axis=1)]
    unnamed x23 -> x24, local copies, waits for them, and re-layouts: 2.61 us -> 0.3 us
  transfers between devices with their start and end apart: 2 -> 0, of which waited for: 2 -> 0; matrix products, arithmetic and copies ran while one was open for 3% -> 0% of each run, Pallas kernels for 0% -> 0%
where the time goes in v2:
time: 66.1 us; the launch traced here: 65.9 us
  Pallas kernels  60.3 us (91%)
  local copies, waits for them, and re-layouts  4.87 us (7%)
  between operations  0.8 us (1%)
    pallas_call x1, Pallas kernels, on_device(): pl.pallas_call(functools.partial(correlate, bands, slabs, slab, depth, wi...  60.3 us
    reshape x1, local copies, waits for them, and re-layouts, on_device(): templates.reshape(count, TMPL, TMPL, TMPL)  2.66 us

profile of v2, /device:TPU:13, one launch (start us, length us, event | category | flops | bytes accessed | tf_op | source)
XLA Modules:
  0.0 65.9 jit_solution(7588092170155185599)
XLA Ops:
  0.6 2.7 %reshape.17 = bf16[2,48,48,48]{3,2,1,0:T(8,128)(2,1)S(1)} reshape(bf16[2,48,2304]{2,1,0:T(8,128)(2,1)} %param.15) | data formatting | bytes 884736 | tf_op jit(solution)/shard_map/reshape | solution.py:330
  3.3 0.2 pad.8
  3.5 0.0 copy-start.11
  3.5 0.0 copy-start
  3.6 0.0 copy-start.1
  3.6 0.0 copy-start.2
  3.6 0.0 copy-start.3
  3.6 0.0 copy-start.4
  3.6 0.0 copy-start.5
  3.6 0.0 copy-start.6
  3.6 0.0 copy-start.7
  3.6 0.0 copy-start.8
  3.7 0.0 copy-start.9
  3.7 0.0 copy-start.10
  3.7 0.8 %reshape.18.t_ref = bf16[2,48,3072]{2,1,0:T(8,128)(2,1)S(1)} reshape(bf16[2,48,48,64]{3,2,1,0:T(8,128)(2,1)S(1)} %pad.8) | data formatting | bytes 1179648 | tf_op jit(solution)/shard_map/reshape | solution.py:331
  4.5 0.0 copy-done.11
  4.5 0.1 broadcast_in_dim.2.fac_ref
  4.6 0.1 copy-done
  4.7 0.0 copy-done.1
  4.7 0.1 copy-done.2
  4.8 0.0 copy-done.3
  4.8 0.0 copy-done.4
  4.8 0.0 copy-done.5
  4.8 0.0 copy-done.6
  4.8 0.0 copy-done.7
  4.8 0.0 copy-done.8
  4.8 0.0 copy-done.9
  4.8 0.0 copy-done.10
  4.9 60.3 %correlate.1 = (f32[384,128]{1,0:T(8,128)S(1)}, f32[384,128]{1,0:T(8,128)S(1)}) custom-call(bf16[24,128,128]{2,1,0:T(8,128)(2,1)S(1)} %copy-done, bf16[2,48,3072]{2,1,0:T(8,128)(2,1)S(1)} %reshape.18.t_ref, f32[8,128]{1,0:T(8,128)S(1)} %broadcast_in_dim.2.fac_ref, bf16[256,256]{1,0:T(8,128)(2,1)S(1)} %copy-done.1, bf16[256,256]{1,0:T(8,128)(2,1)S(1)} %copy-done.3, ...), custom_call_target="tpu_custom_call" | custom-call | tf_op jit(solution)/shard_map/correlate/pallas_call | solution.py:340
  65.1 0.8 %copy_bitcast_fusion = (f32[24,16,128]{2,1,0:T(8,128)}, f32[24,16,128]{2,1,0:T(8,128)}) fusion(f32[16,24,128]{2,1,0:T(8,128)S(1)} %bitcast.9, f32[16,24,128]{2,1,0:T(8,128)S(1)} %bitcast.8), kind=kLoop, calls=%fused_computation | loop fusion | bytes 786432 | tf_op jit(solution)/shard_map/transpose | solution.py:369
  (2 shorter events, 0.0 us)
Async XLA Ops:
  3.5 0.9 %copy-start.11 = (s32[2]{0:T(128)S(1)}, s32[2]{0:T(128)}, u32[]{:S(2)}) copy-start(s32[2]{0:T(128)} %param.16) | copy-start | bytes 28
  3.5 1.1 %copy-start = (bf16[24,128,128]{2,1,0:T(8,128)(2,1)S(1)}, bf16[24,128,128]{2,1,0:T(8,128)(2,1)}, u32[]{:S(2)}) copy-start(bf16[24,128,128]{2,1,0:T(8,128)(2,1)} %tom.1) | copy-start | bytes 2359300
  3.6 1.1 %copy-start.1 = (bf16[256,256]{1,0:T(8,128)(2,1)S(1)}, bf16[256,256]{1,0:T(8,128)(2,1)}, u32[]{:S(2)}) copy-start(bf16[256,256]{1,0:T(8,128)(2,1)} %constant.32.clone.fx.iy) | copy-start | bytes 393220
  3.6 1.2 %copy-start.2 = (bf16[256,512]{1,0:T(8,128)(2,1)S(1)}, bf16[256,512]{1,0:T(8,128)(2,1)}, u32[]{:S(2)}) copy-start(bf16[256,512]{1,0:T(8,128)(2,1)} %constant.37.clone.tx) | copy-start | bytes 786436
  3.6 1.2 %copy-start.3 = (bf16[256,256]{1,0:T(8,128)(2,1)S(1)}, bf16[256,256]{1,0:T(8,128)(2,1)}, u32[]{:S(2)}) copy-start(bf16[256,256]{1,0:T(8,128)(2,1)} %constant.33.clone.fy) | copy-start | bytes 393220
  3.6 1.2 %copy-start.4 = (bf16[256,128]{1,0:T(8,128)(2,1)S(1)}, bf16[256,128]{1,0:T(8,128)(2,1)}, u32[]{:S(2)}) copy-start(bf16[256,128]{1,0:T(8,128)(2,1)} %constant.34.clone.ix) | copy-start | bytes 196612
  3.6 1.2 %copy-start.5 = (bf16[256,96]{1,0:T(8,128)(2,1)S(1)}, bf16[256,96]{1,0:T(8,128)(2,1)}, u32[]{:S(2)}) copy-start(bf16[256,96]{1,0:T(8,128)(2,1)} %constant.38.clone.ty) | copy-start | bytes 147460
  3.6 1.2 %copy-start.6 = (bf16[256,128]{1,0:T(8,128)(2,1)S(1)}, bf16[256,128]{1,0:T(8,128)(2,1)}, u32[]{:S(2)}) copy-start(bf16[256,128]{1,0:T(8,128)(2,1)} %constant.41.clone.bx) | copy-start | bytes 196612
  3.6 1.2 %copy-start.7 = (bf16[96,48]{1,0:T(8,128)(2,1)S(1)}, bf16[96,48]{1,0:T(8,128)(2,1)}, u32[]{:S(2)}) copy-start(bf16[96,48]{1,0:T(8,128)(2,1)} %constant.36.clone.tz) | copy-start | bytes 27652
  3.6 1.2 %copy-start.8 = (bf16[80,72]{1,0:T(8,128)(2,1)S(1)}, bf16[80,72]{1,0:T(8,128)(2,1)}, u32[]{:S(2)}) copy-start(bf16[80,72]{1,0:T(8,128)(2,1)} %constant.35.clone.fz) | copy-start | bytes 34564
  3.7 1.2 %copy-start.9 = (bf16[48,80]{1,0:T(8,128)(2,1)S(1)}, bf16[48,80]{1,0:T(8,128)(2,1)}, u32[]{:S(2)}) copy-start(bf16[48,80]{1,0:T(8,128)(2,1)} %constant.39.clone.iz) | copy-start | bytes 23044
  3.7 1.2 %copy-start.10 = (bf16[24,144]{1,0:T(8,128)(2,1)S(1)}, bf16[24,144]{1,0:T(8,128)(2,1)}, u32[]{:S(2)}) copy-start(bf16[24,144]{1,0:T(8,128)(2,1)} %constant.40.clone.bz) | copy-start | bytes 20740

commit v3 on v2

--- a/solution.py
+++ b/solution.py
@@ -12,6 +12,8 @@
 TMPL = 48
 HALF = TMPL // 2
 KP = 40
+LINE = 2 * KP + 8
+WIDE = 2 * TMPL + 8
 CUBE = 64
 BF16 = jnp.bfloat16
 F32 = jnp.float32
@@ -80,14 +82,22 @@
     bands, slabs, slab, depth, window,
     tom, t_ref, fac_ref, fx, fy, iy, ix, fz, tz, tx, ty, iz, bz, bx,
     best_ref, orient_ref,
-    halo, block, stage, spec, cube, wide, lines, rows_e, inv_ref, corr, got, facs,
-    halo_send, halo_recv, send, recv, send_f, recv_f,
+    halo, block, stage, spec, cube, padded, wide, lines, rows_iy, other, rows_e, inv_ref, corr, got, facs,
+    halo_send, halo_recv, send, recv, send_f, recv_f, send_t, recv_t,
 ):
     pairs = KP // 2
     band_rows = window // bands
     count = t_ref.shape[0]
     me = lax.axis_index("rot")
     at_slab = lax.axis_index("slab")
+    half = bands // 2
+    side = me // half
+    place = lax.rem(me, half)
+    partner = lax.rem(me + half, bands)
+    half_rows = window // 2
+    odd = lax.rem(at_slab, 2)
+    sibling = at_slab + 1 - 2 * odd
+    share = count // 2
     has_left, has_right = at_slab > 0, at_slab < slabs - 1
     mesh_ids = pl.DeviceIdType.MESH
 
@@ -132,12 +142,23 @@
         )
 
     def score_copy(d, r):
-        peer = lax.rem(me + d, bands)
+        spot = lax.rem(place + d, half)
+        peer = side * half + spot
         return pltpu.make_async_remote_copy(
-            src_ref=corr.at[peer, r], dst_ref=got.at[d, r],
+            src_ref=corr.at[spot, r], dst_ref=got.at[d, r],
             send_sem=send.at[r, d], recv_sem=recv.at[r, d],
             device_id={"rot": peer}, device_id_type=mesh_ids,
         )
+
+    def template_copy(hop):
+        mine = pl.ds(odd * share, share)
+        return pltpu.make_async_remote_copy(
+            src_ref=(other if hop else t_ref).at[mine], dst_ref=other.at[mine],
+            send_sem=send_t.at[hop], recv_sem=recv_t.at[hop],
+            device_id={"slab": sibling} if hop else {"rot": partner}, device_id_type=mesh_ids,
+        )
+
+    template_copy(0).start()
 
     @pl.when(has_right)
     def _():
@@ -152,19 +173,26 @@
     facs[0] = fac_ref[...]
 
     chunks = TMPL * CUBE // window
-    for r in range(count):
-        for c in range(chunks):
-            out = dot(tz[...], t_ref[r, :, c * window : (c + 1) * window]).astype(BF16)
-            cube[c * TMPL : (c + 1) * TMPL, :window] = out[:TMPL]
-            cube[c * TMPL : (c + 1) * TMPL, window:] = out[TMPL:]
-        for c in range(chunks):
-            out = dot(cube[c * TMPL : (c + 1) * TMPL, :], tx[...])
-            for e in range(2):
-                for p in range(2):
-                    at = (2 * e + p) * window
-                    wide[r, pl.ds(p * TMPL + 2 * c + e, KP, stride=2 * TMPL), :] = out[
-                        :KP, at : at + window
-                    ]
+    padded[...] = jnp.zeros_like(padded)
+
+    def prepare(source):
+        for r in range(count):
+            for y in range(TMPL):
+                padded[:, y * CUBE : y * CUBE + TMPL] = source[r, :, y * TMPL : (y + 1) * TMPL]
+            for c in range(chunks):
+                out = dot(tz[...], padded[:, c * window : (c + 1) * window]).astype(BF16)
+                cube[c * TMPL : (c + 1) * TMPL, :window] = out[:TMPL]
+                cube[c * TMPL : (c + 1) * TMPL, window:] = out[TMPL:]
+            for c in range(chunks):
+                out = dot(cube[c * TMPL : (c + 1) * TMPL, :], tx[...])
+                for e in range(2):
+                    for p in range(2):
+                        at = (2 * e + p) * window
+                        wide[r, pl.ds(p * TMPL + 2 * c + e, KP, stride=WIDE), :] = out[
+                            :KP, at : at + window
+                        ]
+
+    prepare(t_ref)
 
     @pl.loop(0, slab)
     def _(z):
@@ -186,12 +214,12 @@
     def _():
         to_left().wait_recv()
 
-    for side, there, first in ((0, has_left, 0), (1, has_right, HALF + slab)):
+    for which, there, first in ((0, has_left, 0), (1, has_right, HALF + slab)):
         @pl.when(there)
         def _():
             @pl.loop(0, HALF)
             def _(z):
-                block[pl.ds(first + z, window, stride=depth), :] = halo[side, z].astype(F32)
+                block[pl.ds(first + z, window, stride=depth), :] = halo[which, z].astype(F32)
 
         @pl.when(jnp.logical_not(there))
         def _():
@@ -209,12 +237,15 @@
         )
         out = dot(fz[...], several.astype(BF16))
         for j in range(group):
-            stage[pl.ds(y + j, 2 * KP, stride=window), :] = out[:, j * window : (j + 1) * window]
+            stage[pl.ds(y + j, 2 * KP, stride=window + 8), :] = out[:, j * window : (j + 1) * window]
+
+    template_copy(0).wait()
+    template_copy(1).start()
 
     @pl.loop(0, pairs, unroll=4)
     def _(i):
         def plane(k):
-            return cast_rows(stage, k * window, window)
+            return cast_rows(stage, k * (window + 8), window)
 
         top = jnp.concatenate([plane(2 * i), plane(KP + 2 * i)], axis=1)
         low = jnp.concatenate([plane(2 * i + 1), plane(KP + 2 * i + 1)], axis=1)
@@ -223,12 +254,23 @@
         right = jnp.concatenate([out[window:, :window], out[window:, window:]], axis=0)
         spec[i] = dot(fy[...], jnp.concatenate([left, right], axis=1)).astype(BF16)
 
-    for r in range(count):
+    first_row = pl.multiple_of(side * half_rows, half_rows)
+    inverse = jnp.concatenate(
+        [iy[pl.ds(first_row, half_rows), :], iy[pl.ds(window + first_row, half_rows), :]], axis=0
+    )
+    rows_iy[...] = inverse
+
+    for rr in range(2 * count):
+        r = rr % count
+        if rr == count:
+            template_copy(1).wait()
+            prepare(other)
+
         @pl.loop(0, pairs, unroll=2)
         def _(i):
-            at = pl.multiple_of(i * (4 * TMPL), 4 * TMPL)
+            at = pl.multiple_of(i * (2 * WIDE), 16)
             rhs = jnp.concatenate(
-                [wide[r, pl.ds(at, 2 * TMPL), :], wide[r, pl.ds(at + 2 * TMPL, 2 * TMPL), :]],
+                [wide[r, pl.ds(at, 2 * TMPL), :], wide[r, pl.ds(at + WIDE, 2 * TMPL), :]],
                 axis=1,
             ).astype(BF16)
             temp = dot(ty[...], rhs).astype(BF16).astype(F32)
@@ -236,33 +278,33 @@
             tr, ti = temp[:window], temp[window:]
             sr, si = freq[:window], freq[window:]
             prod = jnp.concatenate([sr * tr - si * ti, sr * ti + si * tr], axis=0).astype(BF16)
-            out = dot(iy[...], prod)
+            out = dot(rows_iy[...], prod)
             for e in range(2):
                 for p in range(2):
-                    lines[pl.ds(p * KP + 2 * i + e, window, stride=2 * KP), :] = out[
-                        p * window : (p + 1) * window, e * window : (e + 1) * window
+                    lines[pl.ds(p * KP + 2 * i + e, half_rows, stride=LINE), :] = out[
+                        p * half_rows : (p + 1) * half_rows, e * window : (e + 1) * window
                     ]
 
-        @pl.loop(1, bands + 1)
+        @pl.loop(1, half + 1)
         def _(d):
-            b = lax.rem(me + d, bands)
+            b = lax.rem(place + d, half)
             parts = []
             for j in range(band_rows // 2):
-                at = (b * band_rows + 2 * j) * (2 * KP)
+                at = (b * band_rows + 2 * j) * LINE
                 rhs = jnp.concatenate(
-                    [cast_rows(lines, at, 2 * KP), cast_rows(lines, at + 2 * KP, 2 * KP)], axis=1
+                    [cast_rows(lines, at, 2 * KP), cast_rows(lines, at + LINE, 2 * KP)], axis=1
                 ).astype(BF16)
                 out = dot(iz[...], rhs)
                 for e in range(2):
                     one = out[:, e * window : (e + 1) * window]
                     parts.append(jnp.concatenate([one[:slab], one[slab:]], axis=1))
-            corr[b, r] = dot(jnp.concatenate(parts, axis=0).astype(BF16), ix[...]).astype(BF16)
-
-            @pl.when(d < bands)
+            corr[b, rr] = dot(jnp.concatenate(parts, axis=0).astype(BF16), ix[...]).astype(BF16)
+
+            @pl.when(d < half)
             def _():
-                score_copy(d, r).start()
-
-    got[0] = corr[me]
+                score_copy(d, rr).start()
+
+    got[0] = corr[place]
 
     reach = band_rows + TMPL - 1
 
@@ -290,8 +332,8 @@
 
     for d in range(1, bands):
         factor_copy(d).wait()
-    for r in range(count):
-        for d in range(1, bands):
+    for r in range(2 * count):
+        for d in range(1, half):
             score_copy(d, r).wait()
     rows = inv_ref.shape[0]
     step = 32
@@ -301,18 +343,20 @@
         at = pl.ds(pl.multiple_of(i * step, step), step)
         inv = inv_ref[at, :]
         best = None
-        for d in range(bands):
-            for r in range(count):
+        for d in range(half):
+            for r in range(2 * count):
                 value = got[d, r, at, :].astype(F32) * inv
                 best = value if best is None else jnp.maximum(best, value)
         total = jnp.zeros_like(best)
         moment = jnp.zeros_like(best)
-        for d in range(bands):
-            for r in range(count):
+        for d in range(half):
+            source = side * half + lax.rem(place + half - d, half)
+            for r in range(2 * count):
+                owner = lax.rem(me - source + bands + (r // count) * half, bands)
                 value = got[d, r, at, :].astype(F32) * inv
                 weight = jnp.square(jnp.maximum(value - best + 1.0, 0.0))
                 total = total + weight
-                moment = moment + weight * facs[d, r : r + 1, :]
+                moment = moment + weight * facs[owner, r % count : r % count + 1, :]
         best_ref[at, :] = best
         orient_ref[at, :] = moment / total
 
@@ -326,9 +370,6 @@
     depth = slab + TMPL
     bands, slabs = lax.axis_size("rot"), lax.axis_size("slab")
     band_rows = window // bands
-    cubes = jnp.pad(
-        templates.reshape(count, TMPL, TMPL, TMPL), ((0, 0), (0, 0), (0, 0), (0, CUBE - TMPL))
-    ).reshape(count, TMPL, TMPL * CUBE)
     pairs = KP // 2
     factors = 1.0 - (2.0 * rotation_ids.astype(F32) + 1.0) / (count * bands)
     fac_rows = 8 * pl.cdiv(count, 8)
@@ -345,25 +386,28 @@
         scratch_shapes=[
             pltpu.VMEM((2, HALF, window, window), BF16),
             pltpu.VMEM((window * depth, window), F32),
-            pltpu.VMEM((2 * KP * window, window), F32),
+            pltpu.VMEM((2 * KP * (window + 8), window), F32),
             pltpu.VMEM((pairs, 2 * window, 2 * window), BF16),
             pltpu.VMEM((TMPL * CUBE // window * TMPL, 2 * window), BF16),
-            pltpu.VMEM((count, KP * 2 * TMPL, window), F32),
-            pltpu.VMEM((window * 2 * KP, window), F32),
+            pltpu.VMEM((TMPL, TMPL * CUBE), BF16),
+            pltpu.VMEM((count, KP * WIDE, window), F32),
+            pltpu.VMEM((window // 2 * LINE, window), F32),
+            pltpu.VMEM((window, 2 * window), BF16),
+            pltpu.VMEM((count, TMPL, TMPL * TMPL), BF16),
             pltpu.VMEM((band_rows + TMPL - 1, slab, window), F32),
             pltpu.VMEM((rows, window), F32),
-            pltpu.VMEM((bands, count, rows, window), BF16),
-            pltpu.VMEM((bands, count, rows, window), BF16),
+            pltpu.VMEM((bands // 2, 2 * count, rows, window), BF16),
+            pltpu.VMEM((bands // 2, 2 * count, rows, window), BF16),
             pltpu.VMEM((bands, fac_rows, window), F32),
             dma((2,)), dma((2,)),
-            dma((count, bands)), dma((count, bands)),
-            dma((bands,)), dma((bands,)),
+            dma((2 * count, bands // 2)), dma((2 * count, bands // 2)),
+            dma((bands,)), dma((bands,)), dma((2,)), dma((2,)),
         ],
         compiler_params=pltpu.CompilerParams(
             collective_id=0, has_side_effects=True, vmem_limit_bytes=50 * 2**20
         ),
         name="correlate",
-    )(tomogram, cubes, factors, *tables(depth, slab, window))
+    )(tomogram, templates, factors, *tables(depth, slab, window))
 
     def placed(a):
         return jnp.swapaxes(a.reshape(band_rows, slab, window), 0, 1)

time: 66.1 us -> 73.1 us (1.11); the launches traced: 65.9 us -> 72.1 us
  local copies, waits for them, and re-layouts: 4.87 us -> 10.5 us
    unnamed x24, local copies, waits for them, and re-layouts: 0.3 us -> 9.6 us
    reshape x2 -> x0, local copies, waits for them, and re-layouts: 3.45 us -> none  [the longest x1 2.66 us: on_device(): templates.reshape(count, TMPL, TMPL, TMPL)]
where the time goes in v3:
time: 73.1 us; the launch traced here: 72.1 us
  Pallas kernels  60.3 us (82%)
  local copies, waits for them, and re-layouts  10.5 us (14%)
    pallas_call x1, Pallas kernels, on_device(): pl.pallas_call(functools.partial(correlate, bands, slabs, slab, depth, wi...  60.3 us
    unnamed x24, local copies, waits for them, and re-layouts  9.6 us

profile of v3, /device:TPU:13, one launch (start us, length us, event | category | flops | bytes accessed | tf_op | source)
XLA Modules:
  0.0 72.1 jit_solution(2627680503836339811)
XLA Ops:
  0.6 0.0 copy-start.10
  0.6 0.7 multiply_subtract_fusion
  1.3 0.1 broadcast_in_dim.2.fac_ref
  1.4 0.0 copy-done.10
  1.4 0.0 copy-start
  1.4 1.1 %copy-done = bf16[24,128,128]{2,1,0:T(8,128)(2,1)S(1)} copy-done((bf16[24,128,128]{2,1,0:T(8,128)(2,1)S(1)}, bf16[24,128,128]{2,1,0:T(8,128)(2,1)}, u32[]{:S(2)}) %copy-start) | copy-done | bytes 786456
  2.5 0.0 copy-start.1
  2.5 0.9 %copy-done.1 = bf16[256,256]{1,0:T(8,128)(2,1)S(1)} copy-done((bf16[256,256]{1,0:T(8,128)(2,1)S(1)}, bf16[256,256]{1,0:T(8,128)(2,1)}, u32[]{:S(2)}) %copy-start.1) | copy-done | bytes 131096
  3.4 0.0 copy-start.2
  3.4 1.0 %copy-done.2 = bf16[2,48,2304]{2,1,0:T(8,128)(2,1)S(1)} copy-done((bf16[2,48,2304]{2,1,0:T(8,128)(2,1)S(1)}, bf16[2,48,2304]{2,1,0:T(8,128)(2,1)}, u32[]{:S(2)}) %copy-start.2) | copy-done | bytes 442392
  4.4 0.0 copy-start.3
  4.4 0.9 %copy-done.3 = bf16[256,512]{1,0:T(8,128)(2,1)S(1)} copy-done((bf16[256,512]{1,0:T(8,128)(2,1)S(1)}, bf16[256,512]{1,0:T(8,128)(2,1)}, u32[]{:S(2)}) %copy-start.3) | copy-done | bytes 262168
  5.4 0.0 copy-start.4
  5.4 0.9 %copy-done.4 = bf16[256,256]{1,0:T(8,128)(2,1)S(1)} copy-done((bf16[256,256]{1,0:T(8,128)(2,1)S(1)}, bf16[256,256]{1,0:T(8,128)(2,1)}, u32[]{:S(2)}) %copy-start.4) | copy-done | bytes 131096
  6.3 0.0 copy-start.5
  6.3 0.8 %copy-done.5 = bf16[256,128]{1,0:T(8,128)(2,1)S(1)} copy-done((bf16[256,128]{1,0:T(8,128)(2,1)S(1)}, bf16[256,128]{1,0:T(8,128)(2,1)}, u32[]{:S(2)}) %copy-start.5) | copy-done | bytes 65560
  7.1 0.0 copy-start.6
  7.1 0.8 %copy-done.6 = bf16[256,96]{1,0:T(8,128)(2,1)S(1)} copy-done((bf16[256,96]{1,0:T(8,128)(2,1)S(1)}, bf16[256,96]{1,0:T(8,128)(2,1)}, u32[]{:S(2)}) %copy-start.6) | copy-done | bytes 49176
  8.0 0.0 copy-start.7
  8.0 0.8 %copy-done.7 = bf16[256,128]{1,0:T(8,128)(2,1)S(1)} copy-done((bf16[256,128]{1,0:T(8,128)(2,1)S(1)}, bf16[256,128]{1,0:T(8,128)(2,1)}, u32[]{:S(2)}) %copy-start.7) | copy-done | bytes 65560
  8.8 0.0 copy-start.8
  8.8 0.7 %copy-done.8 = bf16[96,48]{1,0:T(8,128)(2,1)S(1)} copy-done((bf16[96,48]{1,0:T(8,128)(2,1)S(1)}, bf16[96,48]{1,0:T(8,128)(2,1)}, u32[]{:S(2)}) %copy-start.8) | copy-done | bytes 9240
  9.6 0.0 copy-start.9
  9.6 0.7 %copy-done.9 = bf16[80,72]{1,0:T(8,128)(2,1)S(1)} copy-done((bf16[80,72]{1,0:T(8,128)(2,1)S(1)}, bf16[80,72]{1,0:T(8,128)(2,1)}, u32[]{:S(2)}) %copy-start.9) | copy-done | bytes 11544
  10.3 0.0 copy-start.11
  10.3 0.7 copy-done.11
  11.0 60.3 %correlate.1 = (f32[384,128]{1,0:T(8,128)S(1)}, f32[384,128]{1,0:T(8,128)S(1)}) custom-call(bf16[24,128,128]{2,1,0:T(8,128)(2,1)S(1)} %copy-done, bf16[2,48,2304]{2,1,0:T(8,128)(2,1)S(1)} %copy-done.2, f32[8,128]{1,0:T(8,128)S(1)} %broadcast_in_dim.2.fac_ref, bf16[256,256]{1,0:T(8,128)(2,1)S(1)} %copy-done.1, bf16[256,256]{1,0:T(8,128)(2,1)S(1)} %copy-done.4, ...), custom_call_target="tpu_custom_call" | custom-call | tf_op jit(solution)/shard_map/correlate/pallas_call | solution.py:381
  71.3 0.8 %copy_bitcast_fusion = (f32[24,16,128]{2,1,0:T(8,128)}, f32[24,16,128]{2,1,0:T(8,128)}) fusion(f32[16,24,128]{2,1,0:T(8,128)S(1)} %bitcast.7, f32[16,24,128]{2,1,0:T(8,128)S(1)} %bitcast.6), kind=kLoop, calls=%fused_computation | loop fusion | bytes 786432 | tf_op jit(solution)/shard_map/transpose | solution.py:413
  (1 shorter events, 0.0 us)
Async XLA Ops:
  0.6 0.8 %copy-start.10 = (bf16[24,144]{1,0:T(8,128)(2,1)S(1)}, bf16[24,144]{1,0:T(8,128)(2,1)}, u32[]{:S(2)}) copy-start(bf16[24,144]{1,0:T(8,128)(2,1)} %constant.38.clone.bz) | copy-start | bytes 20740
  1.4 1.1 %copy-start = (bf16[24,128,128]{2,1,0:T(8,128)(2,1)S(1)}, bf16[24,128,128]{2,1,0:T(8,128)(2,1)}, u32[]{:S(2)}) copy-start(bf16[24,128,128]{2,1,0:T(8,128)(2,1)} %tom.1) | copy-start | bytes 2359300
  2.5 0.9 %copy-start.1 = (bf16[256,256]{1,0:T(8,128)(2,1)S(1)}, bf16[256,256]{1,0:T(8,128)(2,1)}, u32[]{:S(2)}) copy-start(bf16[256,256]{1,0:T(8,128)(2,1)} %constant.30.clone.fx.iy) | copy-start | bytes 393220
  3.4 1.0 %copy-start.2 = (bf16[2,48,2304]{2,1,0:T(8,128)(2,1)S(1)}, bf16[2,48,2304]{2,1,0:T(8,128)(2,1)}, u32[]{:S(2)}) copy-start(bf16[2,48,2304]{2,1,0:T(8,128)(2,1)} %t_ref.1) | copy-start | bytes 1327108
  4.4 0.9 %copy-start.3 = (bf16[256,512]{1,0:T(8,128)(2,1)S(1)}, bf16[256,512]{1,0:T(8,128)(2,1)}, u32[]{:S(2)}) copy-start(bf16[256,512]{1,0:T(8,128)(2,1)} %constant.35.clone.tx) | copy-start | bytes 786436
  5.4 0.9 %copy-start.4 = (bf16[256,256]{1,0:T(8,128)(2,1)S(1)}, bf16[256,256]{1,0:T(8,128)(2,1)}, u32[]{:S(2)}) copy-start(bf16[256,256]{1,0:T(8,128)(2,1)} %constant.31.clone.fy) | copy-start | bytes 393220
  6.3 0.8 %copy-start.5 = (bf16[256,128]{1,0:T(8,128)(2,1)S(1)}, bf16[256,128]{1,0:T(8,128)(2,1)}, u32[]{:S(2)}) copy-start(bf16[256,128]{1,0:T(8,128)(2,1)} %constant.39.clone.bx) | copy-start | bytes 196612
  7.1 0.8 %copy-start.6 = (bf16[256,96]{1,0:T(8,128)(2,1)S(1)}, bf16[256,96]{1,0:T(8,128)(2,1)}, u32[]{:S(2)}) copy-start(bf16[256,96]{1,0:T(8,128)(2,1)} %constant.36.clone.ty) | copy-start | bytes 147460
  8.0 0.8 %copy-start.7 = (bf16[256,128]{1,0:T(8,128)(2,1)S(1)}, bf16[256,128]{1,0:T(8,128)(2,1)}, u32[]{:S(2)}) copy-start(bf16[256,128]{1,0:T(8,128)(2,1)} %constant.32.clone.ix) | copy-start | bytes 196612
  8.8 0.7 %copy-start.8 = (bf16[96,48]{1,0:T(8,128)(2,1)S(1)}, bf16[96,48]{1,0:T(8,128)(2,1)}, u32[]{:S(2)}) copy-start(bf16[96,48]{1,0:T(8,128)(2,1)} %constant.34.clone.tz) | copy-start | bytes 27652
  9.6 0.7 %copy-start.9 = (bf16[80,72]{1,0:T(8,128)(2,1)S(1)}, bf16[80,72]{1,0:T(8,128)(2,1)}, u32[]{:S(2)}) copy-start(bf16[80,72]{1,0:T(8,128)(2,1)} %constant.33.clone.fz) | copy-start | bytes 34564
  10.3 0.7 copy-start.11

commit v4 on v3

--- a/solution.py
+++ b/solution.py
@@ -62,7 +62,13 @@
     turn = np.mod(np.arange(window)[:, None] - np.arange(window)[None, :] + HALF, window)
     bx = (turn < TMPL).astype(np.float64)
     bx = np.concatenate([bx, bx], 0)
-    return [jnp.asarray(t, BF16) for t in (fx, fy, iy, ix, fz, tz, tx, ty, iz, bz, bx)]
+    pieces, places, row = [], [], 0
+    for t in (fx, fy, iy, ix, fz, tz, tx[:, : 2 * window], tx[:, 2 * window :], ty, iz, bz, bx):
+        tall = -(-t.shape[0] // 16) * 16
+        pieces.append(pad_to(t, tall, 2 * window))
+        places.append((row, tall, t.shape[1]))
+        row += tall
+    return jnp.asarray(np.concatenate(pieces, 0), BF16), places
 
 
 def dot(a, b):
@@ -79,12 +85,15 @@
 
 
 def correlate(
-    bands, slabs, slab, depth, window,
-    tom, t_ref, fac_ref, fx, fy, iy, ix, fz, tz, tx, ty, iz, bz, bx,
+    bands, slabs, slab, depth, window, places,
+    tom, t_ref, fac_ref, table,
     best_ref, orient_ref,
     halo, block, stage, spec, cube, padded, wide, lines, rows_iy, other, rows_e, inv_ref, corr, got, facs,
     halo_send, halo_recv, send, recv, send_f, recv_f, send_t, recv_t,
 ):
+    fx, fy, iy, ix, fz, tz, tx0, tx1, ty, iz, bz, bx = [
+        table.at[pl.ds(row, tall), pl.ds(0, wide_to)] for row, tall, wide_to in places
+    ]
     pairs = KP // 2
     band_rows = window // bands
     count = t_ref.shape[0]
@@ -184,10 +193,10 @@
                 cube[c * TMPL : (c + 1) * TMPL, :window] = out[:TMPL]
                 cube[c * TMPL : (c + 1) * TMPL, window:] = out[TMPL:]
             for c in range(chunks):
-                out = dot(cube[c * TMPL : (c + 1) * TMPL, :], tx[...])
                 for e in range(2):
+                    out = dot(cube[c * TMPL : (c + 1) * TMPL, :], (tx1 if e else tx0)[...])
                     for p in range(2):
-                        at = (2 * e + p) * window
+                        at = p * window
                         wide[r, pl.ds(p * TMPL + 2 * c + e, KP, stride=WIDE), :] = out[
                             :KP, at : at + window
                         ]
@@ -266,14 +275,14 @@
             template_copy(1).wait()
             prepare(other)
 
-        @pl.loop(0, pairs, unroll=2)
+        @pl.loop(0, pairs, unroll=4)
         def _(i):
             at = pl.multiple_of(i * (2 * WIDE), 16)
             rhs = jnp.concatenate(
                 [wide[r, pl.ds(at, 2 * TMPL), :], wide[r, pl.ds(at + WIDE, 2 * TMPL), :]],
                 axis=1,
             ).astype(BF16)
-            temp = dot(ty[...], rhs).astype(BF16).astype(F32)
+            temp = dot(ty[...], rhs)
             freq = spec[i].astype(F32)
             tr, ti = temp[:window], temp[window:]
             sr, si = freq[:window], freq[window:]
@@ -320,7 +329,7 @@
             parts.append(jnp.concatenate(split(value * value), axis=0))
         out = dot(bz[...], jnp.concatenate(parts, axis=1))
         for j in range(together):
-            rows_e[first + j] = out[:, j * window : (j + 1) * window]
+            rows_e[first + j] = out[:slab, j * window : (j + 1) * window]
 
     sums = rows_e[...]
     for step in (1, 2, 4, 8):
@@ -377,11 +386,12 @@
         jnp.pad(factors, (0, fac_rows - count))[:, None], (fac_rows, window)
     )
     rows = band_rows * slab
+    table, places = tables(depth, slab, window)
     dma = pltpu.SemaphoreType.DMA
     best, orient = pl.pallas_call(
-        functools.partial(correlate, bands, slabs, slab, depth, window),
+        functools.partial(correlate, bands, slabs, slab, depth, window, places),
         out_shape=(jax.ShapeDtypeStruct((rows, window), F32),) * 2,
-        in_specs=[VMEM] * 14,
+        in_specs=[VMEM] * 4,
         out_specs=(VMEM, VMEM),
         scratch_shapes=[
             pltpu.VMEM((2, HALF, window, window), BF16),
@@ -407,7 +417,7 @@
             collective_id=0, has_side_effects=True, vmem_limit_bytes=50 * 2**20
         ),
         name="correlate",
-    )(tomogram, templates, factors, *tables(depth, slab, window))
+    )(tomogram, templates, factors, table)
 
     def placed(a):
         return jnp.swapaxes(a.reshape(band_rows, slab, window), 0, 1)

time: 73.1 us -> 63.7 us (0.87)
  local copies, waits for them, and re-layouts: 10.5 us -> 4.31 us
  Pallas kernels: 60.3 us -> 57.5 us
    unnamed x24 -> x6, local copies, waits for them, and re-layouts: 9.6 us -> 3.42 us
    pallas_call x1, Pallas kernels: 60.3 us -> 57.5 us  [on_device(): pl.pallas_call(functools.partial(correlate, bands, slabs, slab, depth, wi...]
where the time goes in v4:
time: 63.7 us; the launch traced here: 63.1 us
  Pallas kernels  57.5 us (90%)
  local copies, waits for them, and re-layouts  4.31 us (7%)
  other arithmetic  0.66 us (1%)
  between operations  0.64 us (1%)
    pallas_call x1, Pallas kernels, on_device(): pl.pallas_call(functools.partial(correlate, bands, slabs, slab, depth, wi...  57.5 us
    unnamed x6, local copies, waits for them, and re-layouts  3.42 us

profile of v4, /device:TPU:13, one launch (start us, length us, event | category | flops | bytes accessed | tf_op | source)
XLA Modules:
  0.0 63.1 jit_solution(11001803758542956855)
XLA Ops:
  0.6 0.7 %multiply_subtract_fusion = f32[2]{0:T(128)S(1)} fusion(s32[2]{0:T(128)} %param.6), kind=kLoop, calls=%fused_computation.2 | loop fusion | flops 10 | bytes 16 | tf_op jit(solution)/shard_map/sub | solution.py:383
  1.3 0.1 broadcast_in_dim.2.fac_ref
  1.4 0.0 copy-start
  1.4 1.3 %copy-done = bf16[2304,256]{1,0:T(8,128)(2,1)S(1)} copy-done((bf16[2304,256]{1,0:T(8,128)(2,1)S(1)}, bf16[2304,256]{1,0:T(8,128)(2,1)}, u32[]{:S(2)}) %copy-start) | copy-done | bytes 1179672
  2.6 0.0 copy-start.1
  2.6 1.1 %copy-done.1 = bf16[24,128,128]{2,1,0:T(8,128)(2,1)S(1)} copy-done((bf16[24,128,128]{2,1,0:T(8,128)(2,1)S(1)}, bf16[24,128,128]{2,1,0:T(8,128)(2,1)}, u32[]{:S(2)}) %copy-start.1) | copy-done | bytes 786456
  3.8 0.0 copy-start.2
  3.8 1.0 %copy-done.2 = bf16[2,48,2304]{2,1,0:T(8,128)(2,1)S(1)} copy-done((bf16[2,48,2304]{2,1,0:T(8,128)(2,1)S(1)}, bf16[2,48,2304]{2,1,0:T(8,128)(2,1)}, u32[]{:S(2)}) %copy-start.2) | copy-done | bytes 442392
  4.8 57.5 %correlate.1 = (f32[384,128]{1,0:T(8,128)S(1)}, f32[384,128]{1,0:T(8,128)S(1)}) custom-call(bf16[24,128,128]{2,1,0:T(8,128)(2,1)S(1)} %copy-done.1, bf16[2,48,2304]{2,1,0:T(8,128)(2,1)S(1)} %copy-done.2, f32[8,128]{1,0:T(8,128)S(1)} %broadcast_in_dim.2.fac_ref, bf16[2304,256]{1,0:T(8,128)(2,1)S(1)} %copy-done), custom_call_target="tpu_custom_call" | custom-call | tf_op jit(solution)/shard_map/correlate/pallas_call | solution.py:391
  62.3 0.8 %copy_bitcast_fusion = (f32[24,16,128]{2,1,0:T(8,128)}, f32[24,16,128]{2,1,0:T(8,128)}) fusion(f32[16,24,128]{2,1,0:T(8,128)S(1)} %bitcast.7, f32[16,24,128]{2,1,0:T(8,128)S(1)} %bitcast.6), kind=kLoop, calls=%fused_computation | loop fusion | bytes 786432 | tf_op jit(solution)/shard_map/transpose | solution.py:423
  (1 shorter events, 0.0 us)
Async XLA Ops:
  1.4 1.3 %copy-start = (bf16[2304,256]{1,0:T(8,128)(2,1)S(1)}, bf16[2304,256]{1,0:T(8,128)(2,1)}, u32[]{:S(2)}) copy-start(bf16[2304,256]{1,0:T(8,128)(2,1)} %constant.12.clone.table) | copy-start | bytes 3538948
  2.6 1.1 %copy-start.1 = (bf16[24,128,128]{2,1,0:T(8,128)(2,1)S(1)}, bf16[24,128,128]{2,1,0:T(8,128)(2,1)}, u32[]{:S(2)}) copy-start(bf16[24,128,128]{2,1,0:T(8,128)(2,1)} %tom.1) | copy-start | bytes 2359300
  3.8 1.0 %copy-start.2 = (bf16[2,48,2304]{2,1,0:T(8,128)(2,1)S(1)}, bf16[2,48,2304]{2,1,0:T(8,128)(2,1)}, u32[]{:S(2)}) copy-start(bf16[2,48,2304]{2,1,0:T(8,128)(2,1)} %t_ref.1) | copy-start | bytes 1327108
